TPU v7x, 128 devices: a whole 4x4x4 slice. The times are simulated.
128 devices in a mesh: cuts: 4 (over y_lo, core), probe: 32 (over z, x, y_hi).
Axes of the slice: x: 4, y: 4 (y_hi: 2, y_lo: 2; y = y_hi * 2 + y_lo), z: 4, core: 2. Of those that a mesh axis runs over, the one named last changes fastest.
Arguments:
- probe_modes: bfloat16 [256, 2, 512, 512], P(('cuts', 'probe')), may hold values from -6 to 6
- probe_corners: int32 [256, 2], P(('cuts', 'probe')), may hold values from 0 to 2047, as said below
- atom_cells: int32 [262144, 2], P(('cuts', 'probe')), may hold values from 0 to 2047, as said below
- atom_bins: int32 [262144, 1], P(('cuts', 'probe')), may hold values from 0 to 3; in each aligned block of 2048 rows (0 to 2047, 2048 to 4095, ...) at most 1024 rows name the same one
- atom_species: int32 [262144], P(('cuts', 'probe')), may hold values from 0 to 3
- species_amp: float32 [4], replicated, may hold values from 0.5 to 3
- species_width: float32 [4], replicated, may hold values from 0.7 to 2
- fresnel: bfloat16 [2, 512, 512], replicated, as said below
Outputs:
- exit_wave: float32 [256, 2, 512, 512], P(('cuts', 'probe'))
Inputs may be any that keep to these rules, and one draw needn't show every extreme that they name: `atom_cells`: the atoms held by the device at index p along probe lie in grid rows p * 64 to (p + 1) * 64 - 1. `atom_bins`: among the 2048 atoms of one device (aligned blocks) no depth slice holds more than 1024. `probe_corners`: the probes held by the device at index q along probe have their first window row in the row block before q, counted round: grid rows ((q - 1) mod 32) * 64 to that plus 64 - 1. `fresnel`: both planes are zero where row and column indices differ by more than 6.
All inputs are finite; a program needn't handle non-finite values.
Results may differ from a plain program's by a relative error of at most 0.015.
Values may be sent and summed in bfloat16 or wider, within the bound.
A program may use at most 256 MiB of HBM per device.

v0:
```python
import jax
import jax.numpy as jnp
from jax import lax
from jax.sharding import PartitionSpec as P

NG = 2048
NSPEC = 4
CAP = 1024


interaction = 0.4


def lookup(species, table):
    onehot = (species[:, None] == jnp.arange(NSPEC, dtype=jnp.int32)[None, :]).astype(jnp.float32)
    return jnp.sum(onehot * table[None, :], axis=1)


def row_profiles(local_row, strength, spread, row_count):
    grid_rows = jnp.arange(row_count, dtype=jnp.float32)
    offset = grid_rows[None, :] - local_row[:, None]
    return strength[:, None] * jnp.exp(-offset * offset / (2.0 * spread[:, None] * spread[:, None]))


def column_profiles(col_pos, spread, col_count):
    grid_cols = jnp.arange(col_count, dtype=jnp.float32)
    offset = grid_cols[None, :] - col_pos[:, None]
    return jnp.exp(-offset * offset / (2.0 * spread[:, None] * spread[:, None]))


def body(
    probe_modes,
    probe_corners,
    atom_cells,
    atom_bins,
    atom_species,
    species_amp,
    species_width,
    fresnel,
):
    slices = lax.axis_size("cuts")
    row_count = NG // lax.axis_size("probe")
    window_size = probe_modes.shape[-1]
    local_row = (atom_cells[:, 0] % row_count).astype(jnp.float32)
    col_pos = atom_cells[:, 1].astype(jnp.float32)
    strength = lookup(atom_species, species_amp)
    spread = lookup(atom_species, species_width)
    bins = atom_bins[:, 0]
    chosen_int = (bins[:, None] == jnp.arange(slices, dtype=jnp.int32)[None, :]).astype(jnp.int32)
    slot_index = jnp.sum((jnp.cumsum(chosen_int, axis=0) - chosen_int) * chosen_int, axis=1)
    flat_index = bins * CAP + slot_index
    fields = jnp.stack([local_row, col_pos, strength, spread], axis=0)
    filler = jnp.zeros((4, slices * CAP), jnp.float32).at[3, :].set(1.0)
    packed = filler.at[:, flat_index].set(fields).reshape(4, slices, CAP)
    arrived = lax.all_to_all(packed, "cuts", split_axis=1, concat_axis=1, tiled=True)
    flat_fields = arrived.reshape(4, -1)
    rows_part = row_profiles(flat_fields[0], flat_fields[2], flat_fields[3], row_count).astype(
        jnp.bfloat16
    )
    right = column_profiles(flat_fields[1], flat_fields[3], NG).astype(jnp.bfloat16)
    summed = jnp.dot(rows_part.T, right, preferred_element_type=jnp.float32)
    potential_tile = summed.astype(jnp.bfloat16)
    field = lax.all_gather(potential_tile, ("cuts", "probe"), axis=0, tiled=True).reshape(
        slices, NG, NG
    )
    field = jnp.concatenate([field, field[:, :window_size, :]], axis=1)
    row_base = jnp.int32(0)
    field = jnp.concatenate([field, field[:, :, :window_size]], axis=2)
    local_rows = (probe_corners[:, 0] + NG) % NG
    local_corners = jnp.stack([local_rows, probe_corners[:, 1]], axis=1)
    waves = probe_modes.astype(jnp.float32)
    for layer_index in range(slices):
        layer_field = field[layer_index]

        def cut_window(corner):
            return lax.dynamic_slice(
                layer_field, (corner[0], corner[1]), (window_size, window_size)
            )

        windows = jax.vmap(cut_window)(local_corners).astype(jnp.float32)
        cosine = jnp.cos(interaction * windows)
        sine = jnp.sin(interaction * windows)
        real_part = waves[:, 0] * cosine - waves[:, 1] * sine
        imag_part = waves[:, 0] * sine + waves[:, 1] * cosine
        passed = jnp.stack([real_part, imag_part], axis=1).astype(jnp.bfloat16)
        left = jnp.einsum("cij,bdjk->bcdik", fresnel, passed, preferred_element_type=jnp.float32)
        half = jnp.stack(
            [left[:, 0, 0] - left[:, 1, 1], left[:, 0, 1] + left[:, 1, 0]], axis=1
        ).astype(jnp.bfloat16)
        right_side = jnp.einsum(
            "bdij,ckj->bcdik", half, fresnel, preferred_element_type=jnp.float32
        )
        waves = jnp.stack(
            [right_side[:, 0, 0] - right_side[:, 1, 1], right_side[:, 1, 0] + right_side[:, 0, 1]],
            axis=1,
        )
    return waves


def solution(mesh):
    return jax.shard_map(
        body,
        mesh=mesh,
        in_specs=(
            P(("cuts", "probe"), None, None, None),
            P(("cuts", "probe"), None),
            P(("cuts", "probe"), None),
            P(("cuts", "probe"), None),
            P(("cuts", "probe")),
            P(),
            P(),
            P(),
        ),
        out_specs=P(("cuts", "probe"), None, None, None),
        check_vma=False,
    )
```

profile of v0, /device:TPU:103, one launch (start us, length us, event | category | flops | bytes accessed | tf_op | source)
XLA Modules:
  0.0 592.1 jit_solution(7218581112836985691)
XLA Ops:
  15.7 6.7 %scatter_fusion = f32[4,4096]{0,1:T(8,128)S(1)} fusion(f32[4,4096]{0,1:T(8,128)S(1)} %copy-done.1, s32[2048]{0:T(1024)S(1)} %bitcast.352, f32[2048,4]{1,0:T(8,128)} %copy.92), kind=kCustom, calls=%fused_computation | custom fusion | bytes 106496 | tf_op jit(solution)/shard_map/scatter | solution.py:54
  23.0 6.9 %all_to_all.5 = f32[4,4,1024]{2,0,1:T(4,128)S(1)} all-to-all(f32[4,4,1024]{2,0,1:T(4,128)S(1)} %copy.93), channel_id=1, replica_groups=mesh['cuts'=4,'probe'=32] {'cuts'}, dimensions={1} | all-to-all | bytes 131072 | tf_op jit(solution)/shard_map/all_to_all | solution.py:55
  30.0 10.0 %fusion.6 = bf16[64,2048]{1,0:T(8,128)(2,1)} fusion(f32[4096]{0:T(1024)S(1)} %multiply_multiply_fusion, f32[4096]{0:T(1024)S(1)} %bitcast.357, f32[4096]{0:T(1024)S(1)} %bitcast.358, f32[4096]{0:T(1024)S(1)} %bitcast.356), kind=kOutput, calls=%fused_computation.34 | convolution fusion | flops 1117388800 | bytes 327680 | tf_op jit(solution)/shard_map/dot_general | solution.py:61
  40.0 2.8 copy.91
  42.8 2.6 convert_element_type.112
  45.6 344.4 %all-gather.2.cloned.1.call-done = bf16[8192,2048]{1,0:T(8,128)(2,1)} async-done(((bf16[64,2048]{1,0:T(8,128)(2,1)}), bf16[8192,2048]{1,0:T(8,128)(2,1)}) %all-gather.2.cloned.1.call-update) | async-done | bytes 33554448 | tf_op jit(solution)/shard_map/all_gather | solution.py:63
  390.0 8.4 %slice.271 = bf16[4,512,2048]{2,1,0:T(8,128)(2,1)} slice(bf16[4,2048,2048]{2,1,0:T(8,128)(2,1)} %bitcast.346), slice={[0:4], [0:512], [0:2048]} | slice | bytes 16777216 | tf_op jit(solution)/shard_map/slice | solution.py:66
  398.4 49.6 %fusion = bf16[4,2560,2560]{2,1,0:T(8,128)(2,1)} fusion(bf16[4,512,2048]{2,1,0:T(8,128)(2,1)} %slice.271, bf16[4,2048,2048]{2,1,0:T(8,128)(2,1)} %bitcast.347), kind=kLoop, calls=%fused_computation.14 | loop fusion | flops 209715200 | bytes 94371840 | tf_op jit(solution)/shard_map/concatenate | solution.py:68
  448.0 35.6 %slice_bitcast_fusion.3 = (bf16[2560,2560]{1,0:T(8,128)(2,1)}, bf16[2560,2560]{1,0:T(8,128)(2,1)}, bf16[2560,2560]{1,0:T(8,128)(2,1)}, bf16[2560,2560]{1,0:T(8,128)(2,1)}) fusion(bf16[4,2560,2560]{2,1,0:T(8,128)(2,1)} %fusion), kind=kLoop, calls=%fused_computation.23 | loop fusion | bytes 104857600 | tf_op jit(solution)/shard_map/squeeze | solution.py:73
  483.6 7.2 %while.5 = (s32[]{:T(128)}, bf16[2560,2560]{1,0:T(8,128)(2,1)}, s32[2,2]{1,0:T(2,128)S(1)}, bf16[2,512,512]{1,2,0:T(8,128)(2,1)S(1)}, s32[]{:T(128)}) while((s32[]{:T(128)}, bf16[2560,2560]{1,0:T(8,128)(2,1)}, s32[2,2]{1,0:T(2,128)S(1)}, bf16[2,512,512]{1,2,0:T(8,128)(2,1)S(1)}, s32[]{:T(128)}) %tuple.86), condition=%wide.while_cond.1, body=%wide.while_body.1.sunk | while | flops 2 | bytes 3145837 | solution.py:76
  484.3 2.6 dynamic-slice_bitcast_fusion.8
  487.9 2.6 dynamic-slice_bitcast_fusion.8
  490.8 9.1 %fusion.58 = (bf16[2,1,512,512]{2,3,1,0:T(8,128)(2,1)S(1)}, bf16[2,1,512,512]{2,3,1,0:T(8,128)(2,1)S(1)}) fusion(bf16[2,512,512]{1,2,0:T(8,128)(2,1)S(1)} %get-tuple-element.24, f32[2,2,512,512]{2,3,1,0:T(8,128)} %convert_element_type.112), kind=kLoop, calls=%fused_computation.127 | loop fusion | flops 5242880 | bytes 7340032 | tf_op jit(solution)/shard_map/convert.22
  500.0 2.4 convolution_bitcast_fusion.7
  505.1 7.4 %while.6 = (s32[]{:T(128)}, bf16[2560,2560]{1,0:T(8,128)(2,1)}, s32[2,2]{1,0:T(2,128)S(1)}, bf16[2,512,512]{1,2,0:T(8,128)(2,1)S(1)}, s32[]{:T(128)}) while((s32[]{:T(128)}, bf16[2560,2560]{1,0:T(8,128)(2,1)}, s32[2,2]{1,0:T(2,128)S(1)}, bf16[2,512,512]{1,2,0:T(8,128)(2,1)S(1)}, s32[]{:T(128)}) %tuple.91), condition=%wide.while_cond.2, body=%wide.while_body.2.sunk | while | flops 2 | bytes 3145837 | solution.py:76
  505.8 2.8 dynamic-slice_bitcast_fusion.9
  509.5 2.8 dynamic-slice_bitcast_fusion.9
  512.5 4.2 convolution_bitcast_fusion.6
  516.8 8.6 %fusion.54 = (bf16[2,1,512,512]{2,3,0,1:T(8,128)(2,1)S(1)}, bf16[2,1,512,512]{2,3,0,1:T(8,128)(2,1)S(1)}) fusion(bf16[2,512,512]{1,2,0:T(8,128)(2,1)S(1)} %get-tuple-element.32, f32[2,2,2,512,512]{3,4,0,2,1:T(8,128)S(1)} %convolution_bitcast_fusion.6), kind=kLoop, calls=%fused_computation.119 | loop fusion | flops 6291456 | bytes 11534336 | tf_op jit(solution)/shard_map/convert.16
  530.6 7.2 %while.7 = (s32[]{:T(128)}, bf16[2560,2560]{1,0:T(8,128)(2,1)}, s32[2,2]{1,0:T(2,128)S(1)}, bf16[2,512,512]{1,2,0:T(8,128)(2,1)S(1)}, s32[]{:T(128)}) while((s32[]{:T(128)}, bf16[2560,2560]{1,0:T(8,128)(2,1)}, s32[2,2]{1,0:T(2,128)S(1)}, bf16[2,512,512]{1,2,0:T(8,128)(2,1)S(1)}, s32[]{:T(128)}) %tuple.92), condition=%wide.while_cond.3, body=%wide.while_body.3.sunk | while | flops 2 | bytes 3145837 | solution.py:76
  531.2 2.7 dynamic-slice_bitcast_fusion.10
  534.8 2.7 dynamic-slice_bitcast_fusion.10
  537.7 4.2 convolution_bitcast_fusion.4
  541.9 8.5 %fusion.49 = (bf16[2,1,512,512]{2,3,0,1:T(8,128)(2,1)S(1)}, bf16[2,1,512,512]{2,3,0,1:T(8,128)(2,1)S(1)}) fusion(bf16[2,512,512]{1,2,0:T(8,128)(2,1)S(1)} %get-tuple-element.40, f32[2,2,2,512,512]{3,4,0,2,1:T(8,128)S(1)} %convolution_bitcast_fusion.4), kind=kLoop, calls=%fused_computation.110 | loop fusion | flops 6291456 | bytes 11534336 | tf_op jit(solution)/shard_map/convert.10
  550.4 2.4 convolution_bitcast_fusion.3
  555.6 7.3 %while.8 = (s32[]{:T(128)}, bf16[2560,2560]{1,0:T(8,128)(2,1)}, s32[2,2]{1,0:T(2,128)S(1)}, bf16[2,512,512]{1,2,0:T(8,128)(2,1)S(1)}, s32[]{:T(128)}) while((s32[]{:T(128)}, bf16[2560,2560]{1,0:T(8,128)(2,1)}, s32[2,2]{1,0:T(2,128)S(1)}, bf16[2,512,512]{1,2,0:T(8,128)(2,1)S(1)}, s32[]{:T(128)}) %tuple.93), condition=%wide.while_cond.4, body=%wide.while_body.4.sunk | while | flops 2 | bytes 3145837 | solution.py:76
  556.2 2.6 dynamic-slice_bitcast_fusion.11
  559.7 2.6 dynamic-slice_bitcast_fusion.11
  562.8 4.2 convolution_bitcast_fusion.2
  567.1 8.5 %fusion.44 = (bf16[2,1,512,512]{2,3,0,1:T(8,128)(2,1)S(1)}, bf16[2,1,512,512]{2,3,0,1:T(8,128)(2,1)S(1)}) fusion(bf16[2,512,512]{1,2,0:T(8,128)(2,1)S(1)} %get-tuple-element.48, f32[2,2,2,512,512]{3,4,0,2,1:T(8,128)S(1)} %convolution_bitcast_fusion.2), kind=kLoop, calls=%fused_computation.101 | loop fusion | flops 6291456 | bytes 11534336 | tf_op jit(solution)/shard_map/convert.4
  578.7 2.4 convolution_bitcast_fusion
  582.6 2.5 copy.118
  (74 shorter events, 32.4 us)
Async XLA Ops:
  6.5 493.4 %copy-start = (bf16[2,512,512]{2,1,0:T(8,128)(2,1)S(1)}, bf16[2,512,512]{2,1,0:T(8,128)(2,1)}, u32[]{:S(2)}) copy-start(bf16[2,512,512]{2,1,0:T(8,128)(2,1)} %param.17) | copy-start | bytes 3145732
  6.5 383.5 %all-gather.2.cloned.1.call-start = ((), (), s32[]{:S(2)}) async-start(), calls=%async_computation.1 | async-start | bytes 33816576 | tf_op jit(solution)/shard_map/all_gather | solution.py:63
  14.1 1.6 copy-start.1
  42.8 2.6 copy-start.2
Sparse Core Ops, SparseCore 0:
  40.1 349.8 all-gather.1
where the time goes:
time: 598 us; the launch traced here: 592 us
  waiting for transfers between devices  344 us (58%)
  other arithmetic  103 us (17%)
  local copies, waits for them, and re-layouts  88.5 us (15%)
  matrix products  34.6 us (6%)
  between operations  13.8 us (2%)
  blocking collectives  6.87 us (1%)
    all_gather x1, waiting for transfers between devices, body(): lax.all_gather(potential_tile, ('cuts', 'probe'), axis=0, tiled=True)  344 us
    concatenate x1, other arithmetic, body(): field = jnp.concatenate([field, field[:, :, :window_size]], axis=2)  49.6 us
    another operation x6, other arithmetic  36 us
    squeeze x1, local copies, waits for them, and re-layouts, body(): layer_field = field[layer_index]  35.6 us
    gather x40, local copies, waits for them, and re-layouts  28.5 us
    dot_general x4, matrix products, body(): jnp.einsum('bdij,ckj->bcdik', half, fresnel, preferred_element_type=jnp.f...  15 us
  transfers between devices with their start and end apart: 1, of which 1 were waited for; matrix products, arithmetic and copies ran while one was open for 1% of the time, Pallas kernels for 0%

commit v1 on v0

v1 whole, which is shorter than its diff:
```python
import functools

import jax
import jax.numpy as jnp
from jax import lax
from jax.experimental import pallas as pl
from jax.experimental.pallas import tpu as pltpu
from jax.sharding import PartitionSpec as P

NG = 2048
W = 512
TR = 64
NSPEC = 4
NA = 2048
SLICES = 4
CUTS = 4
PROBE = 32
PB = 2

HALO = 9
LISTS = HALO * CUTS
CH = 128
NCH = NA // CH
BUCKET = 16
FIELDS = 5
PACK = FIELDS * NCH + 16
REACH = 28
CT = 256
PASS = 4
MESH = pl.DeviceIdType.MESH
F32 = jnp.float32
BF16 = jnp.bfloat16

PHASE = 0.4 / 6.283185307179586
COS = (
    0.9999992107823225,
    -19.738980355764074,
    64.92865742103473,
    -85.27162153430963,
    58.79049212015824,
    -21.071105627660344,
)
SIN = (
    6.283184916495432,
    -41.34158923268884,
    81.59994332978887,
    -76.61447253130079,
    41.34288235475198,
    -12.471243535265868,
)


def nn(a, b):
    return lax.dot_general(a, b, (((1,), (0,)), ((), ())), preferred_element_type=F32)


def nt(a, b):
    return lax.dot_general(a, b, (((1,), (1,)), ((), ())), preferred_element_type=F32)


def iota(shape, dim):
    return lax.broadcasted_iota(jnp.int32, shape, dim)


def sort_kernel(cells_ref, bins_ref, species_ref, out_ref):
    before = (iota((CH, CH), 0) < iota((CH, CH), 1)).astype(F32).astype(BF16)
    below = (iota((CH, CH), 1) < iota((CH, CH), 0)).astype(F32).astype(BF16)
    ones = jnp.ones((CH, CH), BF16)
    buckets = iota((CH, CH), 0)
    hots = []
    prefixes = []
    running = jnp.zeros((CH, CH), F32)
    by_lane = jnp.zeros((8, CH), F32)
    for c in range(NCH):
        lanes = slice(c * CH, (c + 1) * CH)
        column = cells_ref[1:2, lanes]
        hot = (buckets == column // BUCKET).astype(F32)
        hot16 = hot.astype(BF16)
        prefixes.append(nn(hot16, before) + running)
        running = running + nn(hot16, ones)
        by_lane = by_lane + nt(ones[:8], hot16)
        hots.append(hot)
    high = jnp.floor(running * (1.0 / 64.0))
    low = running - 64.0 * high
    offset = 64.0 * nn(below, high.astype(BF16)) + nn(below, low.astype(BF16))
    lane_high = jnp.floor(by_lane * (1.0 / 64.0))
    lane_low = by_lane - 64.0 * lane_high
    lane_offset = 64.0 * nn(lane_high.astype(BF16), before) + nn(lane_low.astype(BF16), before)
    sorted_fields = jnp.zeros((FIELDS * NCH, CH), F32)
    for c in range(NCH):
        lanes = slice(c * CH, (c + 1) * CH)
        rank = jnp.sum(hots[c] * (prefixes[c] + offset), axis=0, keepdims=True).astype(jnp.int32)
        row = cells_ref[0:1, lanes] & (TR - 1)
        column = cells_ref[1:2, lanes]
        fields = (row, column // 64, column & 63, species_ref[0:1, lanes], bins_ref[0:1, lanes])
        chosen = (iota((NCH, CH), 0) == rank // CH).astype(F32)
        left = jnp.concatenate([chosen * f.astype(F32) for f in fields], axis=0).astype(BF16)
        right = (buckets == (rank & (CH - 1))).astype(F32).astype(BF16)
        sorted_fields = sorted_fields + nt(left, right)
    top = jnp.floor(lane_offset * (1.0 / 64.0))
    out_ref[0 : FIELDS * NCH, :] = sorted_fields.astype(BF16)
    out_ref[FIELDS * NCH : PACK, :] = jnp.concatenate([top, lane_offset - 64.0 * top], axis=0).astype(BF16)


def gather_kernel(own_ref, out_ref, local_sem, send_sems, recv_sems):
    g = lax.axis_index("cuts")
    q = lax.axis_index("probe")
    barrier = pltpu.get_barrier_semaphore()
    pairs = [(j, r) for j in range(HALO) for r in range(CUTS) if (j, r) != (1, 0)]

    def holder(j, r):
        return lax.rem(g + r, CUTS), lax.rem(q + j - 1 + PROBE, PROBE)

    def reader(j, r):
        return lax.rem(g + r, CUTS), lax.rem(q + 1 - j + PROBE, PROBE)

    for j, r in pairs:
        pl.semaphore_signal(barrier, inc=1, device_id=holder(j, r), device_id_type=MESH)
    local = pltpu.make_async_copy(own_ref, out_ref.at[CUTS + g], local_sem)
    local.start()
    pl.semaphore_wait(barrier, len(pairs))
    sends = []
    for n, (j, r) in enumerate(pairs):
        slot = CUTS * j + g
        copy = pltpu.make_async_remote_copy(
            src_ref=own_ref,
            dst_ref=out_ref.at[slot],
            send_sem=send_sems.at[n],
            recv_sem=recv_sems.at[slot],
            device_id=reader(j, r),
            device_id_type=MESH,
        )
        copy.start()
        sends.append(copy)
    local.wait()
    for n, (j, r) in enumerate(pairs):
        slot = CUTS * j + lax.rem(g + r, CUTS)
        pltpu.make_async_remote_copy(
            src_ref=own_ref,
            dst_ref=out_ref.at[slot],
            send_sem=send_sems.at[n],
            recv_sem=recv_sems.at[slot],
            device_id=reader(j, r),
            device_id_type=MESH,
        ).wait_recv()
    for copy in sends:
        copy.wait_send()


LB = 96
LK = 128
NLB = -(-W // LB)
TPAD = 16
RIGHT_SPANS = ((0, 256), (0, 384), (128, 512), (256, 512))


def compute_kernel(
    corners_ref,
    amp_ref,
    width_ref,
    lists_ref,
    modes_ref,
    fresnel_ref,
    out_ref,
    col_ref,
    fall_ref,
    row_ref,
    str_ref,
    bin_ref,
    off_vec,
    off_ref,
    left_ref,
    right_ref,
    acc_ref,
    pot_ref,
    trans_ref,
    half_ref,
    lw_ref,
    rw0,
    rw1,
    rw2,
    rw3,
    sem,
):
    rws = (rw0, rw1, rw2, rw3)

    def unpack_offsets(i, carry):
        base = FIELDS * NCH
        high = lists_ref[i, base : base + 16, :].astype(F32)
        off_vec[pl.ds(i, 1), :] = (64.0 * high[0:1] + high[8:9]).astype(jnp.int32)
        return carry

    lax.fori_loop(0, LISTS, unpack_offsets, 0)
    copy = pltpu.make_async_copy(off_vec, off_ref, sem)
    copy.start()

    def unpack(i, carry):
        def part(f):
            return lists_ref[i, f * NCH : (f + 1) * NCH, :].astype(F32)

        species = part(3)
        amp = jnp.zeros((NCH, CH), F32)
        width = jnp.zeros((NCH, CH), F32)
        for s in range(NSPEC):
            amp = jnp.where(species == s, amp_ref[s], amp)
            width = jnp.where(species == s, width_ref[s], width)
        rows = pl.ds(pl.multiple_of(i * NCH, NCH), NCH)
        row_ref[rows, :] = part(0)
        col_ref[rows, :] = 64.0 * part(1) + part(2)
        fall_ref[rows, :] = -0.7213475204444817 / (width * width)
        str_ref[rows, :] = amp
        bin_ref[rows, :] = part(4)
        return carry

    lax.fori_loop(0, LISTS, unpack, 0)

    for b in range(NLB):
        n = min(LB, W - b * LB)
        turn = (TPAD - b * LB) % W
        for plane in range(2):
            rows = fresnel_ref[plane, b * LB : b * LB + n, :].astype(F32)
            block = pltpu.roll(rows, turn, 1)[:, :LK]
            if plane == 0:
                lw_ref[b, 0:n, 0:LK] = block.astype(BF16)
                lw_ref[b, LB : LB + n, LK : 2 * LK] = block.astype(BF16)
            else:
                lw_ref[b, 0:n, LK : 2 * LK] = (-block).astype(BF16)
                lw_ref[b, LB : LB + n, 0:LK] = block.astype(BF16)
    for b, (lo, hi) in enumerate(RIGHT_SPANS):
        k = hi - lo
        real = fresnel_ref[0, b * 128 : (b + 1) * 128, lo:hi]
        imag = fresnel_ref[1, b * 128 : (b + 1) * 128, lo:hi]
        rws[b][0:128, 0:k] = real
        rws[b][0:128, k : 2 * k] = -imag
        rws[b][128:256, 0:k] = imag
        rws[b][128:256, k : 2 * k] = real
    trans_ref[...] = jnp.zeros_like(trans_ref)
    copy.wait()

    tiles = W // CT

    def window_tile(n, carry):
        t = lax.rem(n, tiles)
        j = lax.rem(n // tiles, HALO)
        w = n // (tiles * HALO)
        shift = corners_ref[w, 0] & (TR - 1)
        first = (corners_ref[w, 1] + t * CT) & (NG - 1)
        rows = ((iota((TR, 1), 0) + shift) & (TR - 1)).astype(F32)
        columns = ((iota((CT, 1), 0) + first) & (NG - 1)).astype(F32)
        last = first + CT - 1 + REACH
        wraps = first + CT - 1 >= NG
        end_bucket = jnp.where(wraps, last - NG, jnp.minimum(last, NG - 1)) // BUCKET + 1
        start_bucket = jnp.maximum(first - REACH, 0) // BUCKET
        starts = []
        passes = jnp.int32(1)
        for l in range(CUTS):
            i = CUTS * j + l
            start = off_ref[i, start_bucket] // CH
            end = jnp.where(end_bucket >= NG // BUCKET, NA, off_ref[i, jnp.minimum(end_bucket, NG // BUCKET - 1)])
            end = jnp.where(wraps, end + NA, end)
            chunks = jnp.minimum((end + CH - 1) // CH - start, NCH)
            passes = jnp.maximum(passes, (chunks + PASS - 1) // PASS)
            starts.append(start)

        def one_pass(p, carry):
            total = None
            for l in range(CUTS):
                for m in range(PASS):
                    chunk = (starts[l] + p * PASS + m) & (NCH - 1)
                    at = pl.ds((CUTS * j + l) * NCH + chunk, 1)
                    lanes = slice(m * CH, (m + 1) * CH)
                    fall = fall_ref[at, :]
                    far = columns - col_ref[at, :]
                    right_ref[l, :, lanes] = jnp.exp2(far * far * fall).astype(BF16)
                    far = rows - row_ref[at, :]
                    profile = str_ref[at, :] * jnp.exp2(far * far * fall)
                    bins = bin_ref[at, :]
                    for k in range(SLICES):
                        left_ref[l, k * TR : (k + 1) * TR, lanes] = jnp.where(bins == k, profile, 0.0).astype(BF16)
                part = nt(left_ref[l], right_ref[l])
                total = part if total is None else total + part

            @pl.when(p == 0)
            def _():
                acc_ref[...] = total

            @pl.when(p > 0)
            def _():
                acc_ref[...] += total

            return carry

        lax.fori_loop(0, passes, one_pass, 0)
        for k in range(SLICES):
            for tt in range(tiles):

                @pl.when(t == tt)
                def _():
                    pot_ref[w, j, k, :, tt * CT : (tt + 1) * CT] = acc_ref[k * TR : (k + 1) * TR, :].astype(BF16)

        return carry

    lax.fori_loop(0, PB * HALO * tiles, window_tile, 0)

    for w in range(PB):
        out_ref[w] = modes_ref[w].astype(F32)
        shift = corners_ref[w, 0] & (TR - 1)
        upper = iota((TR, W), 0) + shift < TR

        def one_slice(k, carry):
            def transmit(i, carry):
                rows = pl.ds(pl.multiple_of(i * TR, TR), TR)
                window = jnp.where(upper, pot_ref[w, i, k].astype(F32), pot_ref[w, i + 1, k].astype(F32))
                turns = window * PHASE
                turns = turns - jnp.round(turns)
                square = turns * turns
                cosine = jnp.full_like(square, COS[-1])
                sine = jnp.full_like(square, SIN[-1])
                for a, b in zip(COS[-2::-1], SIN[-2::-1]):
                    cosine = cosine * square + a
                    sine = sine * square + b
                sine = sine * turns
                real = out_ref[w, 0, rows, :]
                imag = out_ref[w, 1, rows, :]
                into = pl.ds(pl.multiple_of(i * TR + TPAD, TPAD), TR)
                trans_ref[0, into, :] = (real * cosine - imag * sine).astype(BF16)
                trans_ref[1, into, :] = (real * sine + imag * cosine).astype(BF16)
                return carry

            lax.fori_loop(0, W // TR, transmit, 0)
            for b in range(NLB):
                n = min(LB, W - b * LB)
                rows = slice(b * LB, b * LB + LK)
                both = jnp.concatenate([trans_ref[0, rows, :], trans_ref[1, rows, :]], axis=0)
                product = nn(lw_ref[b], both).astype(BF16)
                half_ref[0, b * LB : b * LB + n, :] = product[0:n]
                half_ref[1, b * LB : b * LB + n, :] = product[LB : LB + n]
            for b, (lo, hi) in enumerate(RIGHT_SPANS):
                both = jnp.concatenate([half_ref[0, :, lo:hi], half_ref[1, :, lo:hi]], axis=1)
                product = nt(both, rws[b][...])
                out_ref[w, 0, :, b * 128 : (b + 1) * 128] = product[:, :128]
                out_ref[w, 1, :, b * 128 : (b + 1) * 128] = product[:, 128:]
            return carry

        lax.fori_loop(0, SLICES, one_slice, 0)


def compute(corners, amp, width, lists, modes, fresnel):
    smem = pl.BlockSpec(memory_space=pltpu.SMEM)
    vmem = pl.BlockSpec(memory_space=pltpu.VMEM)
    field = pltpu.VMEM((LISTS * NCH, CH), F32)
    return pl.pallas_call(
        compute_kernel,
        out_shape=jax.ShapeDtypeStruct((PB, 2, W, W), F32),
        in_specs=[smem, smem, smem, vmem, vmem, vmem],
        out_specs=vmem,
        scratch_shapes=[
            field,
            field,
            field,
            field,
            field,
            pltpu.VMEM((LISTS, CH), jnp.int32),
            pltpu.SMEM((LISTS, CH), jnp.int32),
            pltpu.VMEM((CUTS, SLICES * TR, PASS * CH), BF16),
            pltpu.VMEM((CUTS, CT, PASS * CH), BF16),
            pltpu.VMEM((SLICES * TR, CT), F32),
            pltpu.VMEM((PB, HALO, SLICES, TR, W), BF16),
            pltpu.VMEM((2, TPAD + W + 80, W), BF16),
            pltpu.VMEM((2, W, W), BF16),
            pltpu.VMEM((NLB, 2 * LB, 2 * LK), BF16),
        ]
        + [pltpu.VMEM((256, 2 * (hi - lo)), BF16) for lo, hi in RIGHT_SPANS]
        + [pltpu.SemaphoreType.DMA],
        compiler_params=pltpu.CompilerParams(vmem_limit_bytes=48 * 1024 * 1024),
        name="windows_and_slices",
    )(corners, amp, width, lists, modes, fresnel)


def sort_atoms(cells, bins, species):
    vmem = pl.BlockSpec(memory_space=pltpu.VMEM)
    return pl.pallas_call(
        sort_kernel,
        out_shape=jax.ShapeDtypeStruct((PACK, CH), BF16),
        in_specs=[vmem, vmem, vmem],
        out_specs=vmem,
        name="sort_atoms",
    )(cells, bins, species)


def gather_lists(own):
    return pl.pallas_call(
        gather_kernel,
        out_shape=jax.ShapeDtypeStruct((LISTS, PACK, CH), BF16),
        in_specs=[pl.BlockSpec(memory_space=pltpu.VMEM)],
        out_specs=pl.BlockSpec(memory_space=pl.ANY),
        scratch_shapes=[
            pltpu.SemaphoreType.DMA,
            pltpu.SemaphoreType.DMA((LISTS,)),
            pltpu.SemaphoreType.DMA((LISTS,)),
        ],
        compiler_params=pltpu.CompilerParams(collective_id=0, has_side_effects=True),
        name="gather_lists",
    )(own)


def body(
    probe_modes,
    probe_corners,
    atom_cells,
    atom_bins,
    atom_species,
    species_amp,
    species_width,
    fresnel,
):
    own = sort_atoms(atom_cells.T, atom_bins.T, atom_species.reshape(1, -1))
    lists = gather_lists(own)
    return compute(probe_corners, species_amp, species_width, lists, probe_modes, fresnel)


def solution(mesh):
    return jax.shard_map(
        body,
        mesh=mesh,
        in_specs=(
            P(("cuts", "probe"), None, None, None),
            P(("cuts", "probe"), None),
            P(("cuts", "probe"), None),
            P(("cuts", "probe"), None),
            P(("cuts", "probe")),
            P(),
            P(),
            P(),
        ),
        out_specs=P(("cuts", "probe"), None, None, None),
        check_vma=False,
    )
```

time: 598 us -> 100 us (0.17)
  waiting for transfers between devices: 344 us -> 0 us
  other arithmetic: 103 us -> 0 us
  Pallas kernels: 0 us -> 93.8 us
  local copies, waits for them, and re-layouts: 88.5 us -> 5.96 us
  matrix products: 34.6 us -> 0 us
  between operations: 13.8 us -> 0.02 us
  blocking collectives: 6.87 us -> 0 us
    all_gather x1 -> x0, waiting for transfers between devices: 344 us -> none  [body(): lax.all_gather(potential_tile, ('cuts', 'probe'), axis=0, tiled=True)]
    pallas_call x0 -> x3, Pallas kernels: none -> 93.8 us  [the longest x1 65.6 us: compute(): pl.pallas_call(compute_kernel, out_shape=jax.ShapeDtypeStruct((PB, 2, W,...]
    concatenate x2 -> x0, other arithmetic: 49.7 us -> none  [the longest x1 49.6 us: body(): field = jnp.concatenate([field, field[:, :, :window_size]], axis=2)]
    another operation x8 -> x0, other arithmetic: 36.6 us -> none
    squeeze x1 -> x0, local copies, waits for them, and re-layouts: 35.6 us -> none  [body(): layer_field = field[layer_index]]
    dot_general x9 -> x0, matrix products: 34.6 us -> none  [the longest x4 15 us: body(): jnp.einsum('bdij,ckj->bcdik', half, fresnel, preferred_element_type=jnp.f...]
    gather x40 -> x0, local copies, waits for them, and re-layouts: 28.5 us -> none
    slice x2 -> x0, local copies, waits for them, and re-layouts: 8.42 us -> none  [the longest x1 8.38 us: body(): field = jnp.concatenate([field, field[:, :window_size, :]], axis=1)]
  transfers between devices with their start and end apart: 1 -> 0, of which waited for: 1 -> 0; matrix products, arithmetic and copies ran while one was open for 1% -> 0% of each run, Pallas kernels for 0% -> 0%
where the time goes in v1:
time: 100 us; the launch traced here: 99.8 us
  Pallas kernels  93.8 us (94%)
  local copies, waits for them, and re-layouts  5.96 us (6%)
    pallas_call x1, Pallas kernels, compute(): pl.pallas_call(compute_kernel, out_shape=jax.ShapeDtypeStruct((PB, 2, W,...  65.6 us
    pallas_call x1, Pallas kernels, gather_lists(): pl.pallas_call(gather_kernel, out_shape=jax.ShapeDtypeStruct((LISTS, PACK...  25.5 us
    unnamed x12, local copies, waits for them, and re-layouts  5.96 us
    pallas_call x1, Pallas kernels, sort_atoms(): pl.pallas_call(sort_kernel, out_shape=jax.ShapeDtypeStruct((PACK, CH), BF...  2.75 us

profile of v1, /device:TPU:103, one launch (start us, length us, event | category | flops | bytes accessed | tf_op | source)
XLA Modules:
  0.0 99.8 jit_solution(1780884977213799772)
XLA Ops:
  0.0 2.7 %sort_atoms.1.own_ref = bf16[96,128]{1,0:T(8,128)(2,1)} custom-call(s32[2,2048]{1,0:T(2,128)} %bitcast.3, s32[1,2048]{1,0:T(1,128)} %bitcast.4, s32[1,2048]{1,0:T(1,128)} %bitcast.5), custom_call_target="tpu_custom_call" | custom-call | tf_op jit(solution)/shard_map/sort_atoms/pallas_call | solution.py:382
  2.7 25.5 %gather_lists.1.lists_ref = bf16[36,96,128]{2,1,0:T(8,128)(2,1)} custom-call(bf16[96,128]{1,0:T(8,128)(2,1)} %sort_atoms.1.own_ref), custom_call_target="tpu_custom_call" | custom-call | tf_op jit(solution)/shard_map/gather_lists/pallas_call | solution.py:392
  28.2 0.0 copy-start
  28.3 1.2 %copy-done = bf16[36,96,128]{2,1,0:T(8,128)(2,1)S(1)} copy-done((bf16[36,96,128]{2,1,0:T(8,128)(2,1)S(1)}, bf16[36,96,128]{2,1,0:T(8,128)(2,1)}, u32[]{:S(2)}) %copy-start) | copy-done | bytes 884760
  29.4 0.0 copy-start.1
  29.4 1.6 %copy-done.1 = bf16[2,2,512,512]{3,2,1,0:T(8,128)(2,1)S(1)} copy-done((bf16[2,2,512,512]{3,2,1,0:T(8,128)(2,1)S(1)}, bf16[2,2,512,512]{3,2,1,0:T(8,128)(2,1)}, u32[]{:S(2)}) %copy-start.1) | copy-done | bytes 2097176
  31.0 0.0 copy-start.2
  31.0 1.2 %copy-done.2 = bf16[2,512,512]{2,1,0:T(8,128)(2,1)S(1)} copy-done((bf16[2,512,512]{2,1,0:T(8,128)(2,1)S(1)}, bf16[2,512,512]{2,1,0:T(8,128)(2,1)}, u32[]{:S(2)}) %copy-start.2) | copy-done | bytes 1048600
  32.2 0.0 copy-start.3
  32.2 0.7 copy-done.3
  32.9 0.0 copy-start.4
  32.9 0.7 copy-done.4
  33.6 0.0 copy-start.5
  33.6 0.7 copy-done.5
  34.2 65.6 %windows_and_slices.1 = f32[2,2,512,512]{3,2,1,0:T(8,128)} custom-call(s32[2,2]{1,0:T(2,128)S(1)} %copy-done.3, f32[4]{0:T(128)S(1)} %copy-done.4, f32[4]{0:T(128)S(1)} %copy-done.5, bf16[36,96,128]{2,1,0:T(8,128)(2,1)S(1)} %copy-done, bf16[2,2,512,512]{3,2,1,0:T(8,128)(2,1)S(1)} %copy-done.1, bf16[2,512,512]{2,1,0:T(8,128)(2,1)S(1)} %copy-done.2), custom_call_target="tpu_custom_call" | custom-call | tf_op jit(solution)/shard_map/windows_and_slices/pallas_call | solution.py:352
Async XLA Ops:
  28.2 1.2 %copy-start = (bf16[36,96,128]{2,1,0:T(8,128)(2,1)S(1)}, bf16[36,96,128]{2,1,0:T(8,128)(2,1)}, u32[]{:S(2)}) copy-start(bf16[36,96,128]{2,1,0:T(8,128)(2,1)} %gather_lists.1.lists_ref) | copy-start | bytes 2654212
  29.4 1.6 %copy-start.1 = (bf16[2,2,512,512]{3,2,1,0:T(8,128)(2,1)S(1)}, bf16[2,2,512,512]{3,2,1,0:T(8,128)(2,1)}, u32[]{:S(2)}) copy-start(bf16[2,2,512,512]{3,2,1,0:T(8,128)(2,1)} %modes_ref.1) | copy-start | bytes 6291460
  31.0 1.2 %copy-start.2 = (bf16[2,512,512]{2,1,0:T(8,128)(2,1)S(1)}, bf16[2,512,512]{2,1,0:T(8,128)(2,1)}, u32[]{:S(2)}) copy-start(bf16[2,512,512]{2,1,0:T(8,128)(2,1)} %fresnel_ref.1) | copy-start | bytes 3145732
  32.2 0.7 copy-start.3
  32.9 0.7 copy-start.4
  33.6 0.7 copy-start.5

commit v2 on v1

--- a/solution.py
+++ b/solution.py
@@ -26,6 +26,8 @@
 PACK = FIELDS * NCH + 16
 REACH = 28
 CT = 256
+GAP = 32
+CLIP = 224.0
 PASS = 4
 MESH = pl.DeviceIdType.MESH
 F32 = jnp.float32
@@ -147,6 +149,7 @@
         copy.wait_send()
 
 
+GR = 32
 LB = 96
 LK = 128
 NLB = -(-W // LB)
@@ -155,6 +158,13 @@
 
 
 def compute_kernel(
+    corners_hbm,
+    amp_hbm,
+    width_hbm,
+    lists_hbm,
+    modes_hbm,
+    fresnel_hbm,
+    out_hbm,
     corners_ref,
     amp_ref,
     width_ref,
@@ -169,20 +179,33 @@
     bin_ref,
     off_vec,
     off_ref,
-    left_ref,
-    right_ref,
+    left0,
+    right0,
+    left1,
+    right1,
     acc_ref,
     pot_ref,
-    trans_ref,
-    half_ref,
+    trans0,
+    trans1,
+    half0,
+    half1,
     lw_ref,
     rw0,
     rw1,
     rw2,
     rw3,
     sem,
+    in_sems,
+    out_sems,
 ):
     rws = (rw0, rw1, rw2, rw3)
+    sources = (lists_hbm, corners_hbm, amp_hbm, width_hbm, fresnel_hbm, modes_hbm)
+    targets = (lists_ref, corners_ref, amp_ref, width_ref, fresnel_ref, modes_ref)
+    fetches = [pltpu.make_async_copy(a, b, in_sems.at[n]) for n, (a, b) in enumerate(zip(sources, targets))]
+    for fetch in fetches:
+        fetch.start()
+    for fetch in fetches[:4]:
+        fetch.wait()
 
     def unpack_offsets(i, carry):
         base = FIELDS * NCH
@@ -214,6 +237,113 @@
 
     lax.fori_loop(0, LISTS, unpack, 0)
 
+    copy.wait()
+    tiles = W // CT
+
+    def which(n):
+        w = jnp.where(n >= HALO, 1, 0)
+        return w, n - HALO * w
+
+    def place(w, t):
+        first = (corners_ref[w, 1] + t * CT) & (NG - 1)
+        return first, first + CT > NG
+
+    def chunk_range(w, j, t):
+        first, wraps = place(w, t)
+        last = first + CT - 1 + REACH
+        end_bucket = jnp.where(wraps, last - NG, jnp.minimum(last, NG - 1)) // BUCKET + 1
+        start_bucket = jnp.maximum(first - REACH, 0) // BUCKET
+        starts = []
+        passes = jnp.int32(1)
+        for l in range(CUTS):
+            i = CUTS * j + l
+            start = off_ref[i, start_bucket] // CH
+            end = jnp.where(end_bucket >= NG // BUCKET, NA, off_ref[i, jnp.minimum(end_bucket, NG // BUCKET - 1)])
+            end = jnp.where(wraps, end + NA, end)
+            chunks = jnp.minimum((end + CH - 1) // CH - start, NCH)
+            passes = jnp.maximum(passes, (chunks + PASS - 1) // PASS)
+            starts.append(start)
+        return starts, passes
+
+    def fill(w, j, t, starts, p, left, right):
+        first, wraps = place(w, t)
+        shift = corners_ref[w, 0] & (TR - 1)
+        rows = ((iota((TR, 1), 0) + shift) & (TR - 1)).astype(F32)
+        step = iota((CT, 1), 0)
+        gap = jnp.where(step >= NG - first, GAP, 0)
+        columns = jnp.broadcast_to((step - CT // 2 + gap).astype(F32), (CT, CH)).astype(BF16)
+        origin = (first + CT // 2).astype(F32)
+        beyond = jnp.where(wraps, NG // 2, -1).astype(F32)
+        for l in range(CUTS):
+            for m in range(PASS):
+                chunk = (starts[l] + p * PASS + m) & (NCH - 1)
+                at = pl.ds((CUTS * j + l) * NCH + chunk, 1)
+                c = l * PASS + m
+                fall = fall_ref[at, :]
+                column = col_ref[at, :]
+                column = column - origin + jnp.where(column < beyond, float(NG + GAP), 0.0)
+                column = jnp.clip(column, -CLIP, CLIP)
+                column16 = jnp.broadcast_to(column, (16, CH)).astype(BF16)
+                fall16 = jnp.broadcast_to(fall, (16, CH)).astype(BF16)
+                for s in range(CT // 16):
+                    far = columns[16 * s : 16 * s + 16] - column16
+                    right[c, 16 * s : 16 * s + 16, :] = jnp.exp2(far * far * fall16)
+                far = rows - row_ref[at, :]
+                profile = (str_ref[at, :] * jnp.exp2(far * far * fall)).astype(BF16)
+                bins = jnp.broadcast_to(bin_ref[at, :], (16, CH))
+                for k in range(SLICES):
+                    mask = (bins == k).astype(F32).astype(BF16)
+                    for s in range(TR // 16):
+                        left[c, k * TR + 16 * s : k * TR + 16 * s + 16, :] = profile[16 * s : 16 * s + 16] * mask
+
+    def product(left, right):
+        wide = [jnp.concatenate([ref[c] for c in range(CUTS * PASS)], axis=1) for ref in (left, right)]
+        return nt(*wide)
+
+    def store(w, j, t, value):
+        for k in range(SLICES):
+            pot_ref[w, j, k, :, t * CT : (t + 1) * CT] = value[k * TR : (k + 1) * TR].astype(BF16)
+
+    def window_blocks(n, most):
+        w, j = which(n)
+        values = [product(left, right) for left, right in buffers]
+        for t, (left, right) in enumerate(buffers):
+            starts, passes = chunk_range(w, j, t)
+            most = jnp.maximum(most, passes)
+            fill(w, j, t, starts, 0, left, right)
+        before = which(jnp.maximum(n - 1, 0))
+        for t, value in enumerate(values):
+            store(*before, t, value)
+        return most
+
+    buffers = ((left0, right0), (left1, right1))
+    most = lax.fori_loop(0, PB * HALO, window_blocks, jnp.int32(1))
+    for t, (left, right) in enumerate(buffers):
+        store(PB - 1, HALO - 1, t, product(left, right))
+
+    def crowded(n, carry):
+        w, j = which(n)
+        for t in range(tiles):
+            starts, passes = chunk_range(w, j, t)
+
+            @pl.when(passes > 1)
+            def _():
+                acc_ref[...] = jnp.zeros_like(acc_ref)
+
+                def one_pass(p, carry):
+                    fill(w, j, t, starts, p, left0, right0)
+                    acc_ref[...] += product(left0, right0)
+                    return carry
+
+                lax.fori_loop(0, passes, one_pass, 0)
+                store(w, j, t, acc_ref[...])
+
+        return carry
+
+    lax.fori_loop(0, jnp.where(most > 1, PB * HALO, 0), crowded, 0)
+
+    for fetch in fetches[4:]:
+        fetch.wait()
     for b in range(NLB):
         n = min(LB, W - b * LB)
         turn = (TPAD - b * LB) % W
@@ -234,127 +364,114 @@
         rws[b][0:128, k : 2 * k] = -imag
         rws[b][128:256, 0:k] = imag
         rws[b][128:256, k : 2 * k] = real
-    trans_ref[...] = jnp.zeros_like(trans_ref)
-    copy.wait()
-
-    tiles = W // CT
-
-    def window_tile(n, carry):
-        t = lax.rem(n, tiles)
-        j = lax.rem(n // tiles, HALO)
-        w = n // (tiles * HALO)
-        shift = corners_ref[w, 0] & (TR - 1)
-        first = (corners_ref[w, 1] + t * CT) & (NG - 1)
-        rows = ((iota((TR, 1), 0) + shift) & (TR - 1)).astype(F32)
-        columns = ((iota((CT, 1), 0) + first) & (NG - 1)).astype(F32)
-        last = first + CT - 1 + REACH
-        wraps = first + CT - 1 >= NG
-        end_bucket = jnp.where(wraps, last - NG, jnp.minimum(last, NG - 1)) // BUCKET + 1
-        start_bucket = jnp.maximum(first - REACH, 0) // BUCKET
-        starts = []
-        passes = jnp.int32(1)
-        for l in range(CUTS):
-            i = CUTS * j + l
-            start = off_ref[i, start_bucket] // CH
-            end = jnp.where(end_bucket >= NG // BUCKET, NA, off_ref[i, jnp.minimum(end_bucket, NG // BUCKET - 1)])
-            end = jnp.where(wraps, end + NA, end)
-            chunks = jnp.minimum((end + CH - 1) // CH - start, NCH)
-            passes = jnp.maximum(passes, (chunks + PASS - 1) // PASS)
-            starts.append(start)
-
-        def one_pass(p, carry):
-            total = None
-            for l in range(CUTS):
-                for m in range(PASS):
-                    chunk = (starts[l] + p * PASS + m) & (NCH - 1)
-                    at = pl.ds((CUTS * j + l) * NCH + chunk, 1)
-                    lanes = slice(m * CH, (m + 1) * CH)
-                    fall = fall_ref[at, :]
-                    far = columns - col_ref[at, :]
-                    right_ref[l, :, lanes] = jnp.exp2(far * far * fall).astype(BF16)
-                    far = rows - row_ref[at, :]
-                    profile = str_ref[at, :] * jnp.exp2(far * far * fall)
-                    bins = bin_ref[at, :]
-                    for k in range(SLICES):
-                        left_ref[l, k * TR : (k + 1) * TR, lanes] = jnp.where(bins == k, profile, 0.0).astype(BF16)
-                part = nt(left_ref[l], right_ref[l])
-                total = part if total is None else total + part
-
-            @pl.when(p == 0)
-            def _():
-                acc_ref[...] = total
-
-            @pl.when(p > 0)
-            def _():
-                acc_ref[...] += total
-
-            return carry
-
-        lax.fori_loop(0, passes, one_pass, 0)
-        for k in range(SLICES):
-            for tt in range(tiles):
-
-                @pl.when(t == tt)
-                def _():
-                    pot_ref[w, j, k, :, tt * CT : (tt + 1) * CT] = acc_ref[k * TR : (k + 1) * TR, :].astype(BF16)
-
-        return carry
-
-    lax.fori_loop(0, PB * HALO * tiles, window_tile, 0)
+    trans0[...] = jnp.zeros_like(trans0)
+    trans1[...] = jnp.zeros_like(trans1)
 
     for w in range(PB):
         out_ref[w] = modes_ref[w].astype(F32)
+
+    def transmit(w, k, trans):
         shift = corners_ref[w, 0] & (TR - 1)
-        upper = iota((TR, W), 0) + shift < TR
-
-        def one_slice(k, carry):
-            def transmit(i, carry):
-                rows = pl.ds(pl.multiple_of(i * TR, TR), TR)
-                window = jnp.where(upper, pot_ref[w, i, k].astype(F32), pot_ref[w, i + 1, k].astype(F32))
-                turns = window * PHASE
-                turns = turns - jnp.round(turns)
-                square = turns * turns
-                cosine = jnp.full_like(square, COS[-1])
-                sine = jnp.full_like(square, SIN[-1])
-                for a, b in zip(COS[-2::-1], SIN[-2::-1]):
-                    cosine = cosine * square + a
-                    sine = sine * square + b
-                sine = sine * turns
-                real = out_ref[w, 0, rows, :]
-                imag = out_ref[w, 1, rows, :]
-                into = pl.ds(pl.multiple_of(i * TR + TPAD, TPAD), TR)
-                trans_ref[0, into, :] = (real * cosine - imag * sine).astype(BF16)
-                trans_ref[1, into, :] = (real * sine + imag * cosine).astype(BF16)
-                return carry
-
-            lax.fori_loop(0, W // TR, transmit, 0)
-            for b in range(NLB):
-                n = min(LB, W - b * LB)
-                rows = slice(b * LB, b * LB + LK)
-                both = jnp.concatenate([trans_ref[0, rows, :], trans_ref[1, rows, :]], axis=0)
-                product = nn(lw_ref[b], both).astype(BF16)
-                half_ref[0, b * LB : b * LB + n, :] = product[0:n]
-                half_ref[1, b * LB : b * LB + n, :] = product[LB : LB + n]
-            for b, (lo, hi) in enumerate(RIGHT_SPANS):
-                both = jnp.concatenate([half_ref[0, :, lo:hi], half_ref[1, :, lo:hi]], axis=1)
-                product = nt(both, rws[b][...])
-                out_ref[w, 0, :, b * 128 : (b + 1) * 128] = product[:, :128]
-                out_ref[w, 1, :, b * 128 : (b + 1) * 128] = product[:, 128:]
-            return carry
-
-        lax.fori_loop(0, SLICES, one_slice, 0)
+        upper = iota((GR, W), 0) + shift
+
+        def group(i):
+            block, part = i * GR // TR, i * GR % TR
+            rows = slice(i * GR, (i + 1) * GR)
+            inner = slice(part, part + GR)
+            window = jnp.where(
+                upper + part < TR,
+                pot_ref[w, block, k, inner, :].astype(F32),
+                pot_ref[w, block + 1, k, inner, :].astype(F32),
+            )
+            turns = window * PHASE
+            turns = turns - jnp.round(turns)
+            square = turns * turns
+            cosine = jnp.full_like(square, COS[-1])
+            sine = jnp.full_like(square, SIN[-1])
+            for a, b in zip(COS[-2::-1], SIN[-2::-1]):
+                cosine = cosine * square + a
+                sine = sine * square + b
+            sine = sine * turns
+            real = out_ref[w, 0, rows, :]
+            imag = out_ref[w, 1, rows, :]
+            into = slice(i * GR + TPAD, (i + 1) * GR + TPAD)
+            trans[0, into, :] = (real * cosine - imag * sine).astype(BF16)
+            trans[1, into, :] = (real * sine + imag * cosine).astype(BF16)
+
+        return [functools.partial(group, i) for i in range(W // GR)]
+
+    def propagate(w, trans, half):
+        def left(b):
+            n = min(LB, W - b * LB)
+            rows = slice(b * LB, b * LB + LK)
+            both = jnp.concatenate([trans[0, rows, :], trans[1, rows, :]], axis=0)
+            product = nn(lw_ref[b], both).astype(BF16)
+            half[0, b * LB : b * LB + n, :] = product[0:n]
+            half[1, b * LB : b * LB + n, :] = product[LB : LB + n]
+
+        def right(b):
+            lo, hi = RIGHT_SPANS[b]
+            both = jnp.concatenate([half[0, :, lo:hi], half[1, :, lo:hi]], axis=1)
+            product = nt(both, rws[b][...])
+            out_ref[w, 0, :, b * 128 : (b + 1) * 128] = product[:, :128]
+            out_ref[w, 1, :, b * 128 : (b + 1) * 128] = product[:, 128:]
+
+        pieces = [(1.0, functools.partial(left, b)) for b in range(NLB)]
+        return pieces + [(3.3, functools.partial(right, b)) for b in range(4)]
+
+    def together(pieces, groups):
+        total = sum(cost for cost, _ in pieces)
+        done, at = 0, 0.0
+        for cost, piece in pieces:
+            piece()
+            at += cost
+            until = round(at / total * len(groups))
+            for group in groups[done:until]:
+                group()
+            done = until
+
+    def send(w):
+        return pltpu.make_async_copy(out_ref.at[w], out_hbm.at[w], out_sems.at[w])
+
+    for group in transmit(0, 0, trans0):
+        group()
+
+    def one_slice(k, carry):
+        @pl.when(corners_ref[0, 0] >= 0)
+        def _():
+            together(propagate(0, trans0, half0), transmit(1, k, trans1))
+
+        @pl.when(corners_ref[0, 0] >= 0)
+        def _():
+            together(propagate(1, trans1, half1), transmit(0, k + 1, trans0))
+
+        return carry
+
+    lax.fori_loop(0, SLICES - 1, one_slice, 0)
+    together(propagate(0, trans0, half0), transmit(1, SLICES - 1, trans1))
+    send(0).start()
+    together(propagate(1, trans1, half1), [])
+    send(1).start()
+    for w in range(PB):
+        send(w).wait()
 
 
 def compute(corners, amp, width, lists, modes, fresnel):
-    smem = pl.BlockSpec(memory_space=pltpu.SMEM)
-    vmem = pl.BlockSpec(memory_space=pltpu.VMEM)
+    hbm = pl.BlockSpec(memory_space=pltpu.HBM)
     field = pltpu.VMEM((LISTS * NCH, CH), F32)
     return pl.pallas_call(
         compute_kernel,
         out_shape=jax.ShapeDtypeStruct((PB, 2, W, W), F32),
-        in_specs=[smem, smem, smem, vmem, vmem, vmem],
-        out_specs=vmem,
+        in_specs=[hbm] * 6,
+        out_specs=hbm,
         scratch_shapes=[
+            pltpu.SMEM((PB, 2), jnp.int32),
+            pltpu.SMEM((NSPEC,), F32),
+            pltpu.SMEM((NSPEC,), F32),
+            pltpu.VMEM((LISTS, PACK, CH), BF16),
+            pltpu.VMEM((PB, 2, W, W), BF16),
+            pltpu.VMEM((2, W, W), BF16),
+            pltpu.VMEM((PB, 2, W, W), F32),
             field,
             field,
             field,
@@ -362,17 +479,21 @@
             field,
             pltpu.VMEM((LISTS, CH), jnp.int32),
             pltpu.SMEM((LISTS, CH), jnp.int32),
-            pltpu.VMEM((CUTS, SLICES * TR, PASS * CH), BF16),
-            pltpu.VMEM((CUTS, CT, PASS * CH), BF16),
+            pltpu.VMEM((CUTS * PASS, SLICES * TR, CH), BF16),
+            pltpu.VMEM((CUTS * PASS, CT, CH), BF16),
+            pltpu.VMEM((CUTS * PASS, SLICES * TR, CH), BF16),
+            pltpu.VMEM((CUTS * PASS, CT, CH), BF16),
             pltpu.VMEM((SLICES * TR, CT), F32),
             pltpu.VMEM((PB, HALO, SLICES, TR, W), BF16),
             pltpu.VMEM((2, TPAD + W + 80, W), BF16),
+            pltpu.VMEM((2, TPAD + W + 80, W), BF16),
+            pltpu.VMEM((2, W, W), BF16),
             pltpu.VMEM((2, W, W), BF16),
             pltpu.VMEM((NLB, 2 * LB, 2 * LK), BF16),
         ]
         + [pltpu.VMEM((256, 2 * (hi - lo)), BF16) for lo, hi in RIGHT_SPANS]
-        + [pltpu.SemaphoreType.DMA],
-        compiler_params=pltpu.CompilerParams(vmem_limit_bytes=48 * 1024 * 1024),
+        + [pltpu.SemaphoreType.DMA, pltpu.SemaphoreType.DMA((6,)), pltpu.SemaphoreType.DMA((PB,))],
+        compiler_params=pltpu.CompilerParams(vmem_limit_bytes=60 * 1024 * 1024),
         name="windows_and_slices",
     )(corners, amp, width, lists, modes, fresnel)
 

time: 100 us -> 71.6 us (0.72)
  Pallas kernels: 93.8 us -> 70.3 us
  local copies, waits for them, and re-layouts: 5.96 us -> 0 us
    pallas_call x1, Pallas kernels: 65.6 us -> 42 us  [compute(): pl.pallas_call(compute_kernel, out_shape=jax.ShapeDtypeStruct((PB, 2, W,...]
    unnamed x12 -> x0, local copies, waits for them, and re-layouts: 5.96 us -> none
where the time goes in v2:
time: 71.6 us; the launch traced here: 70.4 us
  Pallas kernels  70.3 us (98%)
    pallas_call x1, Pallas kernels, compute(): pl.pallas_call(compute_kernel, out_shape=jax.ShapeDtypeStruct((PB, 2, W,...  42 us
    pallas_call x1, Pallas kernels, gather_lists(): pl.pallas_call(gather_kernel, out_shape=jax.ShapeDtypeStruct((LISTS, PACK...  25.5 us
    pallas_call x1, Pallas kernels, sort_atoms(): pl.pallas_call(sort_kernel, out_shape=jax.ShapeDtypeStruct((PACK, CH), BF...  2.75 us

profile of v2, /device:TPU:103, one launch (start us, length us, event | category | flops | bytes accessed | tf_op | source)
XLA Modules:
  0.0 70.4 jit_solution(8000975435953782296)
XLA Ops:
  0.0 2.7 %sort_atoms.1.own_ref = bf16[96,128]{1,0:T(8,128)(2,1)} custom-call(s32[2,2048]{1,0:T(2,128)} %bitcast.3, s32[1,2048]{1,0:T(1,128)} %bitcast.4, s32[1,2048]{1,0:T(1,128)} %bitcast.5), custom_call_target="tpu_custom_call" | custom-call | tf_op jit(solution)/shard_map/sort_atoms/pallas_call | solution.py:503
  2.7 25.5 %gather_lists.1.lists_hbm = bf16[36,96,128]{2,1,0:T(8,128)(2,1)} custom-call(bf16[96,128]{1,0:T(8,128)(2,1)} %sort_atoms.1.own_ref), custom_call_target="tpu_custom_call" | custom-call | tf_op jit(solution)/shard_map/gather_lists/pallas_call | solution.py:513
  28.2 42.0 %windows_and_slices.1 = f32[2,2,512,512]{3,2,1,0:T(8,128)} custom-call(s32[2,2]{1,0:T(2,128)} %corners_hbm.1, f32[4]{0:T(128)} %amp_hbm.1, f32[4]{0:T(128)} %width_hbm.1, bf16[36,96,128]{2,1,0:T(8,128)(2,1)} %gather_lists.1.lists_hbm, bf16[2,2,512,512]{3,2,1,0:T(8,128)(2,1)} %modes_hbm.1, bf16[2,512,512]{2,1,0:T(8,128)(2,1)} %fresnel_hbm.1), custom_call_target="tpu_custom_call" | custom-call | tf_op jit(solution)/shard_map/windows_and_slices/pallas_call | solution.py:462

commit v3 on v2

--- a/solution.py
+++ b/solution.py
@@ -24,7 +24,7 @@
 BUCKET = 16
 FIELDS = 5
 PACK = FIELDS * NCH + 16
-REACH = 28
+REACH = 13.7
 CT = 256
 GAP = 32
 CLIP = 224.0
@@ -64,7 +64,7 @@
     return lax.broadcasted_iota(jnp.int32, shape, dim)
 
 
-def sort_kernel(cells_ref, bins_ref, species_ref, out_ref):
+def sort_into(cells_ref, bins_ref, species_ref, out_ref):
     before = (iota((CH, CH), 0) < iota((CH, CH), 1)).astype(F32).astype(BF16)
     below = (iota((CH, CH), 1) < iota((CH, CH), 0)).astype(F32).astype(BF16)
     ones = jnp.ones((CH, CH), BF16)
@@ -104,11 +104,13 @@
     out_ref[FIELDS * NCH : PACK, :] = jnp.concatenate([top, lane_offset - 64.0 * top], axis=0).astype(BF16)
 
 
-def gather_kernel(own_ref, out_ref, local_sem, send_sems, recv_sems):
+def lists_kernel(cells_ref, bins_ref, species_ref, out_ref, own_ref, local_sem, send_sems, pass_sems, recv_sems):
     g = lax.axis_index("cuts")
     q = lax.axis_index("probe")
+    core = lax.rem(g, 2)
+    sibling = (g + 1 - 2 * core, q)
     barrier = pltpu.get_barrier_semaphore()
-    pairs = [(j, r) for j in range(HALO) for r in range(CUTS) if (j, r) != (1, 0)]
+    pairs = [(j, r) for j in (1, 2, 0, 3, 4, 5, 6, 7, 8) for r in (0, 2) if (j, r) != (1, 0)]
 
     def holder(j, r):
         return lax.rem(g + r, CUTS), lax.rem(q + j - 1 + PROBE, PROBE)
@@ -116,37 +118,42 @@
     def reader(j, r):
         return lax.rem(g + r, CUTS), lax.rem(q + 1 - j + PROBE, PROBE)
 
+    def remote(src, slot, send_sem, device):
+        return pltpu.make_async_remote_copy(
+            src_ref=src,
+            dst_ref=out_ref.at[slot],
+            send_sem=send_sem,
+            recv_sem=recv_sems.at[slot],
+            device_id=device,
+            device_id_type=MESH,
+        )
+
+    pl.semaphore_signal(barrier, inc=1, device_id=sibling, device_id_type=MESH)
     for j, r in pairs:
         pl.semaphore_signal(barrier, inc=1, device_id=holder(j, r), device_id_type=MESH)
+    sort_into(cells_ref, bins_ref, species_ref, own_ref)
     local = pltpu.make_async_copy(own_ref, out_ref.at[CUTS + g], local_sem)
     local.start()
-    pl.semaphore_wait(barrier, len(pairs))
+    pl.semaphore_wait(barrier, len(pairs) + 1)
     sends = []
     for n, (j, r) in enumerate(pairs):
-        slot = CUTS * j + g
-        copy = pltpu.make_async_remote_copy(
-            src_ref=own_ref,
-            dst_ref=out_ref.at[slot],
-            send_sem=send_sems.at[n],
-            recv_sem=recv_sems.at[slot],
-            device_id=reader(j, r),
-            device_id_type=MESH,
-        )
+        sends.append(remote(own_ref, CUTS * j + g, send_sems.at[n], reader(j, r)))
+    sends.append(remote(own_ref, CUTS + g, pass_sems.at[len(pairs)], sibling))
+    for copy in sends:
         copy.start()
-        sends.append(copy)
-    local.wait()
     for n, (j, r) in enumerate(pairs):
         slot = CUTS * j + lax.rem(g + r, CUTS)
-        pltpu.make_async_remote_copy(
-            src_ref=own_ref,
-            dst_ref=out_ref.at[slot],
-            send_sem=send_sems.at[n],
-            recv_sem=recv_sems.at[slot],
-            device_id=reader(j, r),
-            device_id_type=MESH,
-        ).wait_recv()
+        remote(own_ref, slot, send_sems.at[n], sibling).wait_recv()
+        onward = remote(out_ref.at[slot], slot, pass_sems.at[n], sibling)
+        onward.start()
+        sends.append(onward)
+    for j in range(HALO):
+        for r in (1, 3):
+            slot = CUTS * j + lax.rem(g + r, CUTS)
+            remote(own_ref, slot, send_sems.at[0], sibling).wait_recv()
     for copy in sends:
         copy.wait_send()
+    local.wait()
 
 
 GR = 32
@@ -195,6 +202,7 @@
     rw2,
     rw3,
     sem,
+    busy_ref,
     in_sems,
     out_sems,
 ):
@@ -240,6 +248,11 @@
     copy.wait()
     tiles = W // CT
 
+    widest = width_ref[0]
+    for species in range(1, NSPEC):
+        widest = jnp.maximum(widest, width_ref[species])
+    reach = (widest * REACH).astype(jnp.int32) + 1
+
     def which(n):
         w = jnp.where(n >= HALO, 1, 0)
         return w, n - HALO * w
@@ -250,9 +263,9 @@
 
     def chunk_range(w, j, t):
         first, wraps = place(w, t)
-        last = first + CT - 1 + REACH
+        last = first + CT - 1 + reach
         end_bucket = jnp.where(wraps, last - NG, jnp.minimum(last, NG - 1)) // BUCKET + 1
-        start_bucket = jnp.maximum(first - REACH, 0) // BUCKET
+        start_bucket = jnp.maximum(first - reach, 0) // BUCKET
         starts = []
         passes = jnp.int32(1)
         for l in range(CUTS):
@@ -300,47 +313,54 @@
         wide = [jnp.concatenate([ref[c] for c in range(CUTS * PASS)], axis=1) for ref in (left, right)]
         return nt(*wide)
 
-    def store(w, j, t, value):
+    def own_rows(w):
+        return jnp.broadcast_to(iota((TR, 1), 0) + (corners_ref[w, 0] & (TR - 1)) < TR, (TR, CT))
+
+    def store(w, j, t, value, keep=False):
+        own = own_rows(w)
+        lanes = pl.ds(t * CT, CT) if isinstance(t, int) else pl.ds(pl.multiple_of(t * CT, CT), CT)
         for k in range(SLICES):
-            pot_ref[w, j, k, :, t * CT : (t + 1) * CT] = value[k * TR : (k + 1) * TR].astype(BF16)
-
-    def window_blocks(n, most):
+            new = value[k * TR : (k + 1) * TR].astype(BF16)
+            pot_ref[w, j, k, :, lanes] = jnp.where(own, pot_ref[w, j, k, :, lanes], new)
+            if keep:
+                new = jnp.where(own, new, pot_ref[w, j + 1, k, :, lanes])
+            pot_ref[w, j + 1, k, :, lanes] = new
+
+    def window_blocks(n, count):
         w, j = which(n)
         values = [product(left, right) for left, right in buffers]
         for t, (left, right) in enumerate(buffers):
             starts, passes = chunk_range(w, j, t)
-            most = jnp.maximum(most, passes)
+            busy_ref[count] = tiles * n + t
+            count = count + jnp.where(passes > 1, 1, 0)
             fill(w, j, t, starts, 0, left, right)
         before = which(jnp.maximum(n - 1, 0))
         for t, value in enumerate(values):
             store(*before, t, value)
-        return most
+        return count
 
     buffers = ((left0, right0), (left1, right1))
-    most = lax.fori_loop(0, PB * HALO, window_blocks, jnp.int32(1))
+    count = lax.fori_loop(0, PB * HALO, window_blocks, jnp.int32(0))
     for t, (left, right) in enumerate(buffers):
         store(PB - 1, HALO - 1, t, product(left, right))
 
-    def crowded(n, carry):
-        w, j = which(n)
-        for t in range(tiles):
-            starts, passes = chunk_range(w, j, t)
-
-            @pl.when(passes > 1)
-            def _():
-                acc_ref[...] = jnp.zeros_like(acc_ref)
-
-                def one_pass(p, carry):
-                    fill(w, j, t, starts, p, left0, right0)
-                    acc_ref[...] += product(left0, right0)
-                    return carry
-
-                lax.fori_loop(0, passes, one_pass, 0)
-                store(w, j, t, acc_ref[...])
-
+    def crowded(i, carry):
+        entry = busy_ref[i]
+        w, j = which(entry // tiles)
+        t = entry & (tiles - 1)
+        starts, passes = chunk_range(w, j, t)
+        acc_ref[...] = jnp.zeros_like(acc_ref)
+
+        def one_pass(p, carry):
+            fill(w, j, t, starts, p, left0, right0)
+            acc_ref[...] += product(left0, right0)
+            return carry
+
+        lax.fori_loop(0, passes, one_pass, 0)
+        store(w, j, t, acc_ref[...], keep=True)
         return carry
 
-    lax.fori_loop(0, jnp.where(most > 1, PB * HALO, 0), crowded, 0)
+    lax.fori_loop(0, count, crowded, 0)
 
     for fetch in fetches[4:]:
         fetch.wait()
@@ -370,87 +390,72 @@
     for w in range(PB):
         out_ref[w] = modes_ref[w].astype(F32)
 
-    def transmit(w, k, trans):
-        shift = corners_ref[w, 0] & (TR - 1)
-        upper = iota((GR, W), 0) + shift
-
-        def group(i):
-            block, part = i * GR // TR, i * GR % TR
-            rows = slice(i * GR, (i + 1) * GR)
-            inner = slice(part, part + GR)
-            window = jnp.where(
-                upper + part < TR,
-                pot_ref[w, block, k, inner, :].astype(F32),
-                pot_ref[w, block + 1, k, inner, :].astype(F32),
-            )
-            turns = window * PHASE
-            turns = turns - jnp.round(turns)
-            square = turns * turns
-            cosine = jnp.full_like(square, COS[-1])
-            sine = jnp.full_like(square, SIN[-1])
-            for a, b in zip(COS[-2::-1], SIN[-2::-1]):
-                cosine = cosine * square + a
-                sine = sine * square + b
-            sine = sine * turns
-            real = out_ref[w, 0, rows, :]
-            imag = out_ref[w, 1, rows, :]
-            into = slice(i * GR + TPAD, (i + 1) * GR + TPAD)
-            trans[0, into, :] = (real * cosine - imag * sine).astype(BF16)
-            trans[1, into, :] = (real * sine + imag * cosine).astype(BF16)
-
-        return [functools.partial(group, i) for i in range(W // GR)]
-
-    def propagate(w, trans, half):
-        def left(b):
-            n = min(LB, W - b * LB)
-            rows = slice(b * LB, b * LB + LK)
-            both = jnp.concatenate([trans[0, rows, :], trans[1, rows, :]], axis=0)
-            product = nn(lw_ref[b], both).astype(BF16)
-            half[0, b * LB : b * LB + n, :] = product[0:n]
-            half[1, b * LB : b * LB + n, :] = product[LB : LB + n]
-
-        def right(b):
-            lo, hi = RIGHT_SPANS[b]
-            both = jnp.concatenate([half[0, :, lo:hi], half[1, :, lo:hi]], axis=1)
-            product = nt(both, rws[b][...])
-            out_ref[w, 0, :, b * 128 : (b + 1) * 128] = product[:, :128]
-            out_ref[w, 1, :, b * 128 : (b + 1) * 128] = product[:, 128:]
-
-        pieces = [(1.0, functools.partial(left, b)) for b in range(NLB)]
-        return pieces + [(3.3, functools.partial(right, b)) for b in range(4)]
-
-    def together(pieces, groups):
-        total = sum(cost for cost, _ in pieces)
-        done, at = 0, 0.0
-        for cost, piece in pieces:
-            piece()
-            at += cost
-            until = round(at / total * len(groups))
-            for group in groups[done:until]:
-                group()
-            done = until
+    def transmit(w, k, trans, i):
+        rows = slice(i * GR, (i + 1) * GR)
+        block, part = i * GR // TR, i * GR % TR
+        turns = pot_ref[w, block + 1, k, part : part + GR, :].astype(F32) * PHASE
+        turns = turns - jnp.round(turns)
+        square = turns * turns
+        cosine = jnp.full_like(square, COS[-1])
+        sine = jnp.full_like(square, SIN[-1])
+        for a, b in zip(COS[-2::-1], SIN[-2::-1]):
+            cosine = cosine * square + a
+            sine = sine * square + b
+        sine = sine * turns
+        real = out_ref[w, 0, rows, :]
+        imag = out_ref[w, 1, rows, :]
+        into = slice(i * GR + TPAD, (i + 1) * GR + TPAD)
+        trans[0, into, :] = (real * cosine - imag * sine).astype(BF16)
+        trans[1, into, :] = (real * sine + imag * cosine).astype(BF16)
+
+    def left_product(trans, half, b):
+        n = min(LB, W - b * LB)
+        rows = slice(b * LB, b * LB + LK)
+        both = jnp.concatenate([trans[0, rows, :], trans[1, rows, :]], axis=0)
+        product = nn(lw_ref[b], both).astype(BF16)
+        half[0, b * LB : b * LB + n, :] = product[0:n]
+        half[1, b * LB : b * LB + n, :] = product[LB : LB + n]
+
+    def right_product(w, half, b):
+        lo, hi = RIGHT_SPANS[b]
+        both = jnp.concatenate([half[0, :, lo:hi], half[1, :, lo:hi]], axis=1)
+        product = nt(both, rws[b][...])
+        out_ref[w, 0, :, b * 128 : (b + 1) * 128] = product[:, :128]
+        out_ref[w, 1, :, b * 128 : (b + 1) * 128] = product[:, 128:]
+
+    def stage(right, left):
+        spans = [functools.partial(right_product, *right, b) for b in range(4)] if right else []
+        done = 0
+        for b in range(NLB):
+            if b < len(spans):
+                spans[b]()
+            if left:
+                w, k, trans, half = left
+                until = min(W // GR, -(-(b * LB + LK - TPAD) // GR))
+                for i in range(done, until):
+                    transmit(w, k, trans, i)
+                done = until
+                left_product(trans, half, b)
 
     def send(w):
         return pltpu.make_async_copy(out_ref.at[w], out_hbm.at[w], out_sems.at[w])
 
-    for group in transmit(0, 0, trans0):
-        group()
+    stage(None, (0, 0, trans0, half0))
 
     def one_slice(k, carry):
-        @pl.when(corners_ref[0, 0] >= 0)
+        @pl.when(k < SLICES)
         def _():
-            together(propagate(0, trans0, half0), transmit(1, k, trans1))
-
-        @pl.when(corners_ref[0, 0] >= 0)
+            stage((0, half0), (1, k, trans1, half1))
+
+        @pl.when(k < SLICES - 1)
         def _():
-            together(propagate(1, trans1, half1), transmit(0, k + 1, trans0))
+            stage((1, half1), (0, k + 1, trans0, half0))
 
         return carry
 
-    lax.fori_loop(0, SLICES - 1, one_slice, 0)
-    together(propagate(0, trans0, half0), transmit(1, SLICES - 1, trans1))
+    lax.fori_loop(0, SLICES, one_slice, 0)
     send(0).start()
-    together(propagate(1, trans1, half1), [])
+    stage((1, half1), None)
     send(1).start()
     for w in range(PB):
         send(w).wait()
@@ -484,7 +489,7 @@
             pltpu.VMEM((CUTS * PASS, SLICES * TR, CH), BF16),
             pltpu.VMEM((CUTS * PASS, CT, CH), BF16),
             pltpu.VMEM((SLICES * TR, CT), F32),
-            pltpu.VMEM((PB, HALO, SLICES, TR, W), BF16),
+            pltpu.VMEM((PB, HALO + 1, SLICES, TR, W), BF16),
             pltpu.VMEM((2, TPAD + W + 80, W), BF16),
             pltpu.VMEM((2, TPAD + W + 80, W), BF16),
             pltpu.VMEM((2, W, W), BF16),
@@ -492,37 +497,30 @@
             pltpu.VMEM((NLB, 2 * LB, 2 * LK), BF16),
         ]
         + [pltpu.VMEM((256, 2 * (hi - lo)), BF16) for lo, hi in RIGHT_SPANS]
-        + [pltpu.SemaphoreType.DMA, pltpu.SemaphoreType.DMA((6,)), pltpu.SemaphoreType.DMA((PB,))],
+        + [pltpu.SemaphoreType.DMA, pltpu.SMEM((PB * HALO * 2 + 1,), jnp.int32), pltpu.SemaphoreType.DMA((6,)), pltpu.SemaphoreType.DMA((PB,))],
         compiler_params=pltpu.CompilerParams(vmem_limit_bytes=60 * 1024 * 1024),
         name="windows_and_slices",
     )(corners, amp, width, lists, modes, fresnel)
 
 
-def sort_atoms(cells, bins, species):
+def gather_lists(cells, bins, species):
     vmem = pl.BlockSpec(memory_space=pltpu.VMEM)
+    passed = HALO * 2
     return pl.pallas_call(
-        sort_kernel,
-        out_shape=jax.ShapeDtypeStruct((PACK, CH), BF16),
+        lists_kernel,
+        out_shape=jax.ShapeDtypeStruct((LISTS, PACK, CH), BF16),
         in_specs=[vmem, vmem, vmem],
-        out_specs=vmem,
-        name="sort_atoms",
-    )(cells, bins, species)
-
-
-def gather_lists(own):
-    return pl.pallas_call(
-        gather_kernel,
-        out_shape=jax.ShapeDtypeStruct((LISTS, PACK, CH), BF16),
-        in_specs=[pl.BlockSpec(memory_space=pltpu.VMEM)],
-        out_specs=pl.BlockSpec(memory_space=pl.ANY),
+        out_specs=pl.BlockSpec(memory_space=pltpu.HBM),
         scratch_shapes=[
+            pltpu.VMEM((PACK, CH), BF16),
             pltpu.SemaphoreType.DMA,
-            pltpu.SemaphoreType.DMA((LISTS,)),
+            pltpu.SemaphoreType.DMA((passed,)),
+            pltpu.SemaphoreType.DMA((passed,)),
             pltpu.SemaphoreType.DMA((LISTS,)),
         ],
         compiler_params=pltpu.CompilerParams(collective_id=0, has_side_effects=True),
-        name="gather_lists",
-    )(own)
+        name="sort_and_gather",
+    )(cells, bins, species)
 
 
 def body(
@@ -535,8 +533,7 @@
     species_width,
     fresnel,
 ):
-    own = sort_atoms(atom_cells.T, atom_bins.T, atom_species.reshape(1, -1))
-    lists = gather_lists(own)
+    lists = gather_lists(atom_cells.T, atom_bins.T, atom_species.reshape(1, -1))
     return compute(probe_corners, species_amp, species_width, lists, probe_modes, fresnel)
 
 

time: 71.6 us -> 59.9 us (0.84)
  Pallas kernels: 70.3 us -> 59.1 us
    pallas_call x2 -> x1, Pallas kernels: 28.2 us -> 19 us  [gather_lists(): pl.pallas_call(lists_kernel, out_shape=jax.ShapeDtypeStruct((LISTS, PACK,...]
    pallas_call x1, Pallas kernels: 42 us -> 40.1 us  [compute(): pl.pallas_call(compute_kernel, out_shape=jax.ShapeDtypeStruct((PB, 2, W,...]
where the time goes in v3:
time: 59.9 us; the launch traced here: 59.1 us
  Pallas kernels  59.1 us (99%)
    pallas_call x1, Pallas kernels, compute(): pl.pallas_call(compute_kernel, out_shape=jax.ShapeDtypeStruct((PB, 2, W,...  40.1 us
    pallas_call x1, Pallas kernels, gather_lists(): pl.pallas_call(lists_kernel, out_shape=jax.ShapeDtypeStruct((LISTS, PACK,...  19 us

profile of v3, /device:TPU:103, one launch (start us, length us, event | category | flops | bytes accessed | tf_op | source)
XLA Modules:
  0.0 59.1 jit_solution(17817701241808609328)
XLA Ops:
  0.0 19.0 %sort_and_gather.1.lists_hbm = bf16[36,96,128]{2,1,0:T(8,128)(2,1)} custom-call(s32[2,2048]{1,0:T(2,128)} %bitcast.3, s32[1,2048]{1,0:T(1,128)} %bitcast.4, s32[1,2048]{1,0:T(1,128)} %bitcast.5), custom_call_target="tpu_custom_call" | custom-call | tf_op jit(solution)/shard_map/sort_and_gather/pallas_call | solution.py:509
  19.0 40.1 %windows_and_slices.1 = f32[2,2,512,512]{3,2,1,0:T(8,128)} custom-call(s32[2,2]{1,0:T(2,128)} %corners_hbm.1, f32[4]{0:T(128)} %amp_hbm.1, f32[4]{0:T(128)} %width_hbm.1, bf16[36,96,128]{2,1,0:T(8,128)(2,1)} %sort_and_gather.1.lists_hbm, bf16[2,2,512,512]{3,2,1,0:T(8,128)(2,1)} %modes_hbm.1, bf16[2,512,512]{2,1,0:T(8,128)(2,1)} %fresnel_hbm.1), custom_call_target="tpu_custom_call" | custom-call | tf_op jit(solution)/shard_map/windows_and_slices/pallas_call | solution.py:467

commit v4 on v3

--- a/solution.py
+++ b/solution.py
@@ -22,33 +22,36 @@
 CH = 128
 NCH = NA // CH
 BUCKET = 16
-FIELDS = 5
-PACK = FIELDS * NCH + 16
+FIELDS = 4
+PACK = FIELDS * NCH
+TILES = 2
+UNPACK = 12
 REACH = 13.7
 CT = 256
 GAP = 32
 CLIP = 224.0
 PASS = 4
+HEAD = 176
+TAIL = 128
+SPANS = ((0, HEAD), (0, CT), (0, CT), (TAIL, CT))
 MESH = pl.DeviceIdType.MESH
 F32 = jnp.float32
 BF16 = jnp.bfloat16
 
 PHASE = 0.4 / 6.283185307179586
 COS = (
-    0.9999992107823225,
-    -19.738980355764074,
-    64.92865742103473,
-    -85.27162153430963,
-    58.79049212015824,
-    -21.071105627660344,
+    0.9999590208378119,
+    -19.73094236686191,
+    64.67144177616537,
+    -82.390806311774,
+    45.62105110286101,
 )
 SIN = (
-    6.283184916495432,
-    -41.34158923268884,
-    81.59994332978887,
-    -76.61447253130079,
-    41.34288235475198,
-    -12.471243535265868,
+    6.2831611294861265,
+    -41.3368318308275,
+    81.44770647022538,
+    -74.90941970419655,
+    33.548355145172366,
 )
 
 
@@ -72,7 +75,6 @@
     hots = []
     prefixes = []
     running = jnp.zeros((CH, CH), F32)
-    by_lane = jnp.zeros((8, CH), F32)
     for c in range(NCH):
         lanes = slice(c * CH, (c + 1) * CH)
         column = cells_ref[1:2, lanes]
@@ -80,15 +82,11 @@
         hot16 = hot.astype(BF16)
         prefixes.append(nn(hot16, before) + running)
         running = running + nn(hot16, ones)
-        by_lane = by_lane + nt(ones[:8], hot16)
         hots.append(hot)
     high = jnp.floor(running * (1.0 / 64.0))
     low = running - 64.0 * high
     offset = 64.0 * nn(below, high.astype(BF16)) + nn(below, low.astype(BF16))
-    lane_high = jnp.floor(by_lane * (1.0 / 64.0))
-    lane_low = by_lane - 64.0 * lane_high
-    lane_offset = 64.0 * nn(lane_high.astype(BF16), before) + nn(lane_low.astype(BF16), before)
-    sorted_fields = jnp.zeros((FIELDS * NCH, CH), F32)
+    sorted_fields = jnp.zeros((5 * NCH, CH), F32)
     for c in range(NCH):
         lanes = slice(c * CH, (c + 1) * CH)
         rank = jnp.sum(hots[c] * (prefixes[c] + offset), axis=0, keepdims=True).astype(jnp.int32)
@@ -99,9 +97,9 @@
         left = jnp.concatenate([chosen * f.astype(F32) for f in fields], axis=0).astype(BF16)
         right = (buckets == (rank & (CH - 1))).astype(F32).astype(BF16)
         sorted_fields = sorted_fields + nt(left, right)
-    top = jnp.floor(lane_offset * (1.0 / 64.0))
-    out_ref[0 : FIELDS * NCH, :] = sorted_fields.astype(BF16)
-    out_ref[FIELDS * NCH : PACK, :] = jnp.concatenate([top, lane_offset - 64.0 * top], axis=0).astype(BF16)
+    row, high, low, kind, bins = [sorted_fields[f * NCH : (f + 1) * NCH] for f in range(5)]
+    for f, field in enumerate((row, 64.0 * high + low, kind, bins)):
+        out_ref[f * NCH : (f + 1) * NCH, :] = field.astype(jnp.int32).astype(jnp.int16)
 
 
 def lists_kernel(cells_ref, bins_ref, species_ref, out_ref, own_ref, local_sem, send_sems, pass_sems, recv_sems):
@@ -184,8 +182,8 @@
     row_ref,
     str_ref,
     bin_ref,
-    off_vec,
-    off_ref,
+    count_vec,
+    count_ref,
     left0,
     right0,
     left1,
@@ -215,102 +213,124 @@
     for fetch in fetches[:4]:
         fetch.wait()
 
-    def unpack_offsets(i, carry):
-        base = FIELDS * NCH
-        high = lists_ref[i, base : base + 16, :].astype(F32)
-        off_vec[pl.ds(i, 1), :] = (64.0 * high[0:1] + high[8:9]).astype(jnp.int32)
-        return carry
-
-    lax.fori_loop(0, LISTS, unpack_offsets, 0)
-    copy = pltpu.make_async_copy(off_vec, off_ref, sem)
-    copy.start()
-
-    def unpack(i, carry):
+    widest = width_ref[0]
+    for species in range(1, NSPEC):
+        widest = jnp.maximum(widest, width_ref[species])
+    reach = (widest * REACH).astype(jnp.int32) + 1
+
+    def which(n):
+        w = jnp.where(n >= HALO, 1, 0)
+        return w, n - HALO * w
+
+    def place(w, t):
+        first = (corners_ref[w, 1] + t * CT) & (NG - 1)
+        return first, first + CT > NG
+
+    def buckets_of(w, t):
+        first, wraps = place(w, t)
+        most = jnp.where(wraps, 2 * NG, NG) // BUCKET
+        last = first + CT - 1 + reach
+        return (
+            jnp.maximum(first - reach, 0) // BUCKET,
+            (first + HEAD - reach) // BUCKET,
+            jnp.minimum(last // BUCKET + 1, most),
+            jnp.minimum((first + TAIL + reach + BUCKET - 1) // BUCKET, most),
+        )
+
+    lane = iota((1, CH), 1)
+    edge = jnp.zeros((1, CH), jnp.int32)
+    for n in range(PB * TILES):
+        for kind, bucket in enumerate(buckets_of(n // TILES, n % TILES)):
+            bucket = jnp.where(bucket > NG // BUCKET, bucket - NG // BUCKET, bucket)
+            edge = jnp.where(lane == 4 * kind + n, bucket * BUCKET, edge)
+    edge = jnp.broadcast_to(edge.astype(F32), (NCH, CH))
+    by_tail = iota((NCH, CH), 1) < 8
+
+    def unpack_list(i):
         def part(f):
-            return lists_ref[i, f * NCH : (f + 1) * NCH, :].astype(F32)
-
-        species = part(3)
+            return lists_ref[i, f * NCH : (f + 1) * NCH, :].astype(jnp.int32)
+
+        species = part(2)
         amp = jnp.zeros((NCH, CH), F32)
         width = jnp.zeros((NCH, CH), F32)
         for s in range(NSPEC):
             amp = jnp.where(species == s, amp_ref[s], amp)
             width = jnp.where(species == s, width_ref[s], width)
+        column = part(1).astype(F32)
         rows = pl.ds(pl.multiple_of(i * NCH, NCH), NCH)
-        row_ref[rows, :] = part(0)
-        col_ref[rows, :] = 64.0 * part(1) + part(2)
+        row_ref[rows, :] = part(0).astype(F32)
+        col_ref[rows, :] = column
         fall_ref[rows, :] = -0.7213475204444817 / (width * width)
         str_ref[rows, :] = amp
-        bin_ref[rows, :] = part(4)
+        bin_ref[rows, :] = part(3).astype(F32)
+        tail = jnp.broadcast_to(column[:, CH - 1 : CH], (NCH, CH))
+        head = jnp.broadcast_to(column[:, 0:1], (NCH, CH))
+        below = (jnp.where(by_tail, tail, head) < edge).astype(F32)
+        count_vec[pl.ds(i, 1), :] = jnp.sum(below, axis=0, keepdims=True).astype(jnp.int32)
+
+    def unpack(n, carry):
+        for l in range(UNPACK):
+            unpack_list(UNPACK * n + l)
         return carry
 
-    lax.fori_loop(0, LISTS, unpack, 0)
-
+    lax.fori_loop(0, LISTS // UNPACK, unpack, 0)
+    copy = pltpu.make_async_copy(count_vec, count_ref, sem)
+    copy.start()
     copy.wait()
-    tiles = W // CT
-
-    widest = width_ref[0]
-    for species in range(1, NSPEC):
-        widest = jnp.maximum(widest, width_ref[species])
-    reach = (widest * REACH).astype(jnp.int32) + 1
-
-    def which(n):
-        w = jnp.where(n >= HALO, 1, 0)
-        return w, n - HALO * w
-
-    def place(w, t):
-        first = (corners_ref[w, 1] + t * CT) & (NG - 1)
-        return first, first + CT > NG
-
     def chunk_range(w, j, t):
-        first, wraps = place(w, t)
-        last = first + CT - 1 + reach
-        end_bucket = jnp.where(wraps, last - NG, jnp.minimum(last, NG - 1)) // BUCKET + 1
-        start_bucket = jnp.maximum(first - reach, 0) // BUCKET
+        around = [jnp.where(bucket > NG // BUCKET, NCH, 0) for bucket in buckets_of(w, t)]
         starts = []
-        passes = jnp.int32(1)
+        most = jnp.int32(0)
+        long = jnp.int32(0)
         for l in range(CUTS):
-            i = CUTS * j + l
-            start = off_ref[i, start_bucket] // CH
-            end = jnp.where(end_bucket >= NG // BUCKET, NA, off_ref[i, jnp.minimum(end_bucket, NG // BUCKET - 1)])
-            end = jnp.where(wraps, end + NA, end)
-            chunks = jnp.minimum((end + CH - 1) // CH - start, NCH)
-            passes = jnp.maximum(passes, (chunks + PASS - 1) // PASS)
+            start, head, end, tail = [
+                count_ref[CUTS * j + l, 4 * kind + TILES * w + t] + around[kind] for kind in range(4)
+            ]
+            most = jnp.maximum(most, jnp.minimum(end - start, NCH))
+            short = (start + 1 <= head) & (start + PASS - 1 >= tail)
+            long = jnp.maximum(long, jnp.where(short, 0, 1))
             starts.append(start)
-        return starts, passes
-
-    def fill(w, j, t, starts, p, left, right):
+        return starts, most, long
+
+    def fill(w, j, t, starts, steps, left, right, spans=None):
         first, wraps = place(w, t)
         shift = corners_ref[w, 0] & (TR - 1)
-        rows = ((iota((TR, 1), 0) + shift) & (TR - 1)).astype(F32)
+        rows = jnp.broadcast_to(((iota((TR, 1), 0) + shift) & (TR - 1)).astype(F32), (TR, CH)).astype(BF16)
         step = iota((CT, 1), 0)
         gap = jnp.where(step >= NG - first, GAP, 0)
         columns = jnp.broadcast_to((step - CT // 2 + gap).astype(F32), (CT, CH)).astype(BF16)
         origin = (first + CT // 2).astype(F32)
         beyond = jnp.where(wraps, NG // 2, -1).astype(F32)
         for l in range(CUTS):
-            for m in range(PASS):
-                chunk = (starts[l] + p * PASS + m) & (NCH - 1)
+            for n, m in enumerate(steps):
+                chunk = (starts[l] + m) & (NCH - 1)
                 at = pl.ds((CUTS * j + l) * NCH + chunk, 1)
-                c = l * PASS + m
+                c = l * len(steps) + n
                 fall = fall_ref[at, :]
                 column = col_ref[at, :]
                 column = column - origin + jnp.where(column < beyond, float(NG + GAP), 0.0)
                 column = jnp.clip(column, -CLIP, CLIP)
                 column16 = jnp.broadcast_to(column, (16, CH)).astype(BF16)
                 fall16 = jnp.broadcast_to(fall, (16, CH)).astype(BF16)
-                for s in range(CT // 16):
+                low, high = spans[n] if spans else (0, CT)
+                for s in range(low // 16, high // 16):
                     far = columns[16 * s : 16 * s + 16] - column16
                     right[c, 16 * s : 16 * s + 16, :] = jnp.exp2(far * far * fall16)
-                far = rows - row_ref[at, :]
-                profile = (str_ref[at, :] * jnp.exp2(far * far * fall)).astype(BF16)
-                bins = jnp.broadcast_to(bin_ref[at, :], (16, CH))
+                row16 = jnp.broadcast_to(row_ref[at, :], (16, CH)).astype(BF16)
+                profile = []
+                for s in range(TR // 16):
+                    far = rows[16 * s : 16 * s + 16] - row16
+                    profile.append(jnp.exp2(far * far * fall16))
+                bins = jnp.broadcast_to(bin_ref[at, :], (8, CH))
+                strength = jnp.broadcast_to(str_ref[at, :], (8, CH))
                 for k in range(SLICES):
-                    mask = (bins == k).astype(F32).astype(BF16)
+                    scale = jnp.where(bins == k, strength, 0.0)
+                    scale = jnp.concatenate([scale, scale], axis=0).astype(BF16)
                     for s in range(TR // 16):
-                        left[c, k * TR + 16 * s : k * TR + 16 * s + 16, :] = profile[16 * s : 16 * s + 16] * mask
-
-    def product(left, right):
-        wide = [jnp.concatenate([ref[c] for c in range(CUTS * PASS)], axis=1) for ref in (left, right)]
+                        left[c, k * TR + 16 * s : k * TR + 16 * s + 16, :] = profile[s] * scale
+
+    def product(left, right, chunks=CUTS * PASS):
+        wide = [jnp.concatenate([ref[c] for c in range(chunks)], axis=1) for ref in (left, right)]
         return nt(*wide)
 
     def own_rows(w):
@@ -330,33 +350,41 @@
         w, j = which(n)
         values = [product(left, right) for left, right in buffers]
         for t, (left, right) in enumerate(buffers):
-            starts, passes = chunk_range(w, j, t)
-            busy_ref[count] = tiles * n + t
-            count = count + jnp.where(passes > 1, 1, 0)
-            fill(w, j, t, starts, 0, left, right)
+            starts, most, long = chunk_range(w, j, t)
+            busy_ref[count] = TILES * n + t
+            count = count + jnp.where(most > PASS, 1, long)
+            fill(w, j, t, starts, range(PASS), left, right, SPANS)
         before = which(jnp.maximum(n - 1, 0))
         for t, value in enumerate(values):
             store(*before, t, value)
         return count
 
     buffers = ((left0, right0), (left1, right1))
+    for _, right in buffers:
+        for c in range(CUTS * PASS):
+            low, high = SPANS[c % PASS]
+            if low > 0:
+                right[c, 0:low, :] = jnp.zeros((low, CH), BF16)
+            if high < CT:
+                right[c, high:CT, :] = jnp.zeros((CT - high, CH), BF16)
     count = lax.fori_loop(0, PB * HALO, window_blocks, jnp.int32(0))
     for t, (left, right) in enumerate(buffers):
         store(PB - 1, HALO - 1, t, product(left, right))
 
     def crowded(i, carry):
         entry = busy_ref[i]
-        w, j = which(entry // tiles)
-        t = entry & (tiles - 1)
-        starts, passes = chunk_range(w, j, t)
-        acc_ref[...] = jnp.zeros_like(acc_ref)
-
-        def one_pass(p, carry):
-            fill(w, j, t, starts, p, left0, right0)
-            acc_ref[...] += product(left0, right0)
+        w, j = which(entry // TILES)
+        t = entry & (TILES - 1)
+        starts, most, _ = chunk_range(w, j, t)
+        fill(w, j, t, starts, range(PASS), left0, right0)
+        acc_ref[...] = product(left0, right0)
+
+        def one_more(m, carry):
+            fill(w, j, t, starts, [m], left0, right0)
+            acc_ref[...] += product(left0, right0, CUTS)
             return carry
 
-        lax.fori_loop(0, passes, one_pass, 0)
+        lax.fori_loop(PASS, jnp.maximum(most, PASS), one_more, 0)
         store(w, j, t, acc_ref[...], keep=True)
         return carry
 
@@ -473,7 +501,7 @@
             pltpu.SMEM((PB, 2), jnp.int32),
             pltpu.SMEM((NSPEC,), F32),
             pltpu.SMEM((NSPEC,), F32),
-            pltpu.VMEM((LISTS, PACK, CH), BF16),
+            pltpu.VMEM((LISTS, PACK, CH), jnp.int16),
             pltpu.VMEM((PB, 2, W, W), BF16),
             pltpu.VMEM((2, W, W), BF16),
             pltpu.VMEM((PB, 2, W, W), F32),
@@ -508,11 +536,11 @@
     passed = HALO * 2
     return pl.pallas_call(
         lists_kernel,
-        out_shape=jax.ShapeDtypeStruct((LISTS, PACK, CH), BF16),
+        out_shape=jax.ShapeDtypeStruct((LISTS, PACK, CH), jnp.int16),
         in_specs=[vmem, vmem, vmem],
         out_specs=pl.BlockSpec(memory_space=pltpu.HBM),
         scratch_shapes=[
-            pltpu.VMEM((PACK, CH), BF16),
+            pltpu.VMEM((PACK, CH), jnp.int16),
             pltpu.SemaphoreType.DMA,
             pltpu.SemaphoreType.DMA((passed,)),
             pltpu.SemaphoreType.DMA((passed,)),

time: 59.9 us -> 54.4 us (0.908)
  the two profiles are of different devices: /device:TPU:103 before, /device:TPU:1 now
where the time goes in v4:
time: 54.4 us; the launch traced here: 54.3 us
  Pallas kernels  54.3 us (100%)
    pallas_call x1, Pallas kernels, compute(): pl.pallas_call(compute_kernel, out_shape=jax.ShapeDtypeStruct((PB, 2, W,...  35.9 us
    pallas_call x1, Pallas kernels, gather_lists(): pl.pallas_call(lists_kernel, out_shape=jax.ShapeDtypeStruct((LISTS, PACK,...  18.4 us

profile of v4, /device:TPU:1, one launch (start us, length us, event | category | flops | bytes accessed | tf_op | source)
XLA Modules:
  0.0 54.3 jit_solution(3633255458576618108)
XLA Ops:
  0.0 18.4 %sort_and_gather.1.lists_hbm = s16[36,64,128]{2,1,0:T(8,128)(2,1)} custom-call(s32[2,2048]{1,0:T(2,128)} %bitcast.3, s32[1,2048]{1,0:T(1,128)} %bitcast.4, s32[1,2048]{1,0:T(1,128)} %bitcast.5), custom_call_target="tpu_custom_call" | custom-call | tf_op jit(solution)/shard_map/sort_and_gather/pallas_call | solution.py:537
  18.4 35.9 %windows_and_slices.1 = f32[2,2,512,512]{3,2,1,0:T(8,128)} custom-call(s32[2,2]{1,0:T(2,128)} %corners_hbm.1, f32[4]{0:T(128)} %amp_hbm.1, f32[4]{0:T(128)} %width_hbm.1, s16[36,64,128]{2,1,0:T(8,128)(2,1)} %sort_and_gather.1.lists_hbm, bf16[2,2,512,512]{3,2,1,0:T(8,128)(2,1)} %modes_hbm.1, bf16[2,512,512]{2,1,0:T(8,128)(2,1)} %fresnel_hbm.1), custom_call_target="tpu_custom_call" | custom-call | tf_op jit(solution)/shard_map/windows_and_slices/pallas_call | solution.py:495

commit v5 on v4

--- a/solution.py
+++ b/solution.py
@@ -72,31 +72,29 @@
     below = (iota((CH, CH), 1) < iota((CH, CH), 0)).astype(F32).astype(BF16)
     ones = jnp.ones((CH, CH), BF16)
     buckets = iota((CH, CH), 0)
-    hots = []
+    chunks = [slice(c * CH, (c + 1) * CH) for c in range(NCH)]
+    hots = [(buckets == cells_ref[1:2, lanes] // BUCKET).astype(F32) for lanes in chunks]
+    tall = jnp.concatenate([hot.astype(BF16) for hot in hots], axis=0)
+    sums = nn(tall, jnp.concatenate([before, ones], axis=1))
+    running = jnp.zeros((CH, CH), F32)
     prefixes = []
-    running = jnp.zeros((CH, CH), F32)
-    for c in range(NCH):
-        lanes = slice(c * CH, (c + 1) * CH)
-        column = cells_ref[1:2, lanes]
-        hot = (buckets == column // BUCKET).astype(F32)
-        hot16 = hot.astype(BF16)
-        prefixes.append(nn(hot16, before) + running)
-        running = running + nn(hot16, ones)
-        hots.append(hot)
+    for lanes in chunks:
+        prefixes.append(sums[lanes, :CH] + running)
+        running = running + sums[lanes, CH:]
     high = jnp.floor(running * (1.0 / 64.0))
     low = running - 64.0 * high
     offset = 64.0 * nn(below, high.astype(BF16)) + nn(below, low.astype(BF16))
-    sorted_fields = jnp.zeros((5 * NCH, CH), F32)
-    for c in range(NCH):
-        lanes = slice(c * CH, (c + 1) * CH)
-        rank = jnp.sum(hots[c] * (prefixes[c] + offset), axis=0, keepdims=True).astype(jnp.int32)
+    lefts = []
+    rights = []
+    for lanes, hot, prefix in zip(chunks, hots, prefixes):
+        rank = jnp.sum(hot * (prefix + offset), axis=0, keepdims=True).astype(jnp.int32)
         row = cells_ref[0:1, lanes] & (TR - 1)
         column = cells_ref[1:2, lanes]
         fields = (row, column // 64, column & 63, species_ref[0:1, lanes], bins_ref[0:1, lanes])
         chosen = (iota((NCH, CH), 0) == rank // CH).astype(F32)
-        left = jnp.concatenate([chosen * f.astype(F32) for f in fields], axis=0).astype(BF16)
-        right = (buckets == (rank & (CH - 1))).astype(F32).astype(BF16)
-        sorted_fields = sorted_fields + nt(left, right)
+        lefts.append(jnp.concatenate([chosen * f.astype(F32) for f in fields], axis=0).astype(BF16))
+        rights.append((buckets == (rank & (CH - 1))).astype(F32).astype(BF16))
+    sorted_fields = nt(jnp.concatenate(lefts, axis=1), jnp.concatenate(rights, axis=1))
     row, high, low, kind, bins = [sorted_fields[f * NCH : (f + 1) * NCH] for f in range(5)]
     for f, field in enumerate((row, 64.0 * high + low, kind, bins)):
         out_ref[f * NCH : (f + 1) * NCH, :] = field.astype(jnp.int32).astype(jnp.int16)
@@ -276,7 +274,35 @@
     lax.fori_loop(0, LISTS // UNPACK, unpack, 0)
     copy = pltpu.make_async_copy(count_vec, count_ref, sem)
     copy.start()
+
+    for fetch in fetches[4:]:
+        fetch.wait()
+    for b in range(NLB):
+        n = min(LB, W - b * LB)
+        turn = (TPAD - b * LB) % W
+        for plane in range(2):
+            rows = fresnel_ref[plane, b * LB : b * LB + n, :].astype(F32)
+            block = pltpu.roll(rows, turn, 1)[:, :LK]
+            if plane == 0:
+                lw_ref[b, 0:n, 0:LK] = block.astype(BF16)
+                lw_ref[b, LB : LB + n, LK : 2 * LK] = block.astype(BF16)
+            else:
+                lw_ref[b, 0:n, LK : 2 * LK] = (-block).astype(BF16)
+                lw_ref[b, LB : LB + n, 0:LK] = block.astype(BF16)
+    for b, (lo, hi) in enumerate(RIGHT_SPANS):
+        k = hi - lo
+        real = fresnel_ref[0, b * 128 : (b + 1) * 128, lo:hi]
+        imag = fresnel_ref[1, b * 128 : (b + 1) * 128, lo:hi]
+        rws[b][0:128, 0:k] = real
+        rws[b][0:128, k : 2 * k] = -imag
+        rws[b][128:256, 0:k] = imag
+        rws[b][128:256, k : 2 * k] = real
+    trans0[...] = jnp.zeros_like(trans0)
+    trans1[...] = jnp.zeros_like(trans1)
+
+    out_ref[1] = modes_ref[1].astype(F32)
     copy.wait()
+
     def chunk_range(w, j, t):
         around = [jnp.where(bucket > NG // BUCKET, NCH, 0) for bucket in buckets_of(w, t)]
         starts = []
@@ -330,7 +356,7 @@
                         left[c, k * TR + 16 * s : k * TR + 16 * s + 16, :] = profile[s] * scale
 
     def product(left, right, chunks=CUTS * PASS):
-        wide = [jnp.concatenate([ref[c] for c in range(chunks)], axis=1) for ref in (left, right)]
+        wide = [jnp.concatenate([ref[c, 0:CT, :] for c in range(chunks)], axis=1) for ref in (left, right)]
         return nt(*wide)
 
     def own_rows(w):
@@ -390,35 +416,7 @@
 
     lax.fori_loop(0, count, crowded, 0)
 
-    for fetch in fetches[4:]:
-        fetch.wait()
-    for b in range(NLB):
-        n = min(LB, W - b * LB)
-        turn = (TPAD - b * LB) % W
-        for plane in range(2):
-            rows = fresnel_ref[plane, b * LB : b * LB + n, :].astype(F32)
-            block = pltpu.roll(rows, turn, 1)[:, :LK]
-            if plane == 0:
-                lw_ref[b, 0:n, 0:LK] = block.astype(BF16)
-                lw_ref[b, LB : LB + n, LK : 2 * LK] = block.astype(BF16)
-            else:
-                lw_ref[b, 0:n, LK : 2 * LK] = (-block).astype(BF16)
-                lw_ref[b, LB : LB + n, 0:LK] = block.astype(BF16)
-    for b, (lo, hi) in enumerate(RIGHT_SPANS):
-        k = hi - lo
-        real = fresnel_ref[0, b * 128 : (b + 1) * 128, lo:hi]
-        imag = fresnel_ref[1, b * 128 : (b + 1) * 128, lo:hi]
-        rws[b][0:128, 0:k] = real
-        rws[b][0:128, k : 2 * k] = -imag
-        rws[b][128:256, 0:k] = imag
-        rws[b][128:256, k : 2 * k] = real
-    trans0[...] = jnp.zeros_like(trans0)
-    trans1[...] = jnp.zeros_like(trans1)
-
-    for w in range(PB):
-        out_ref[w] = modes_ref[w].astype(F32)
-
-    def transmit(w, k, trans, i):
+    def transmit(w, k, trans, i, waves):
         rows = slice(i * GR, (i + 1) * GR)
         block, part = i * GR // TR, i * GR % TR
         turns = pot_ref[w, block + 1, k, part : part + GR, :].astype(F32) * PHASE
@@ -430,8 +428,8 @@
             cosine = cosine * square + a
             sine = sine * square + b
         sine = sine * turns
-        real = out_ref[w, 0, rows, :]
-        imag = out_ref[w, 1, rows, :]
+        real = waves[w, 0, rows, :].astype(F32)
+        imag = waves[w, 1, rows, :].astype(F32)
         into = slice(i * GR + TPAD, (i + 1) * GR + TPAD)
         trans[0, into, :] = (real * cosine - imag * sine).astype(BF16)
         trans[1, into, :] = (real * sine + imag * cosine).astype(BF16)
@@ -451,24 +449,27 @@
         out_ref[w, 0, :, b * 128 : (b + 1) * 128] = product[:, :128]
         out_ref[w, 1, :, b * 128 : (b + 1) * 128] = product[:, 128:]
 
-    def stage(right, left):
+    def stage(right, left, waves=out_ref, then=None):
         spans = [functools.partial(right_product, *right, b) for b in range(4)] if right else []
         done = 0
         for b in range(NLB):
             if b < len(spans):
                 spans[b]()
+                if then:
+                    then(b)
             if left:
                 w, k, trans, half = left
                 until = min(W // GR, -(-(b * LB + LK - TPAD) // GR))
                 for i in range(done, until):
-                    transmit(w, k, trans, i)
+                    transmit(w, k, trans, i, waves)
                 done = until
                 left_product(trans, half, b)
 
-    def send(w):
-        return pltpu.make_async_copy(out_ref.at[w], out_hbm.at[w], out_sems.at[w])
-
-    stage(None, (0, 0, trans0, half0))
+    def send(w, b):
+        lanes = slice(b * 128, (b + 1) * 128)
+        return pltpu.make_async_copy(out_ref.at[w, :, :, lanes], out_hbm.at[w, :, :, lanes], out_sems.at[w, b])
+
+    stage(None, (0, 0, trans0, half0), waves=modes_ref)
 
     def one_slice(k, carry):
         @pl.when(k < SLICES)
@@ -482,11 +483,12 @@
         return carry
 
     lax.fori_loop(0, SLICES, one_slice, 0)
-    send(0).start()
-    stage((1, half1), None)
-    send(1).start()
+    for b in range(4):
+        send(0, b).start()
+    stage((1, half1), None, then=lambda b: send(1, b).start())
     for w in range(PB):
-        send(w).wait()
+        for b in range(4):
+            send(w, b).wait()
 
 
 def compute(corners, amp, width, lists, modes, fresnel):
@@ -512,10 +514,10 @@
             field,
             pltpu.VMEM((LISTS, CH), jnp.int32),
             pltpu.SMEM((LISTS, CH), jnp.int32),
-            pltpu.VMEM((CUTS * PASS, SLICES * TR, CH), BF16),
-            pltpu.VMEM((CUTS * PASS, CT, CH), BF16),
-            pltpu.VMEM((CUTS * PASS, SLICES * TR, CH), BF16),
-            pltpu.VMEM((CUTS * PASS, CT, CH), BF16),
+            pltpu.VMEM((CUTS * PASS, SLICES * TR + 16, CH), BF16),
+            pltpu.VMEM((CUTS * PASS, CT + 16, CH), BF16),
+            pltpu.VMEM((CUTS * PASS, SLICES * TR + 16, CH), BF16),
+            pltpu.VMEM((CUTS * PASS, CT + 16, CH), BF16),
             pltpu.VMEM((SLICES * TR, CT), F32),
             pltpu.VMEM((PB, HALO + 1, SLICES, TR, W), BF16),
             pltpu.VMEM((2, TPAD + W + 80, W), BF16),
@@ -525,7 +527,7 @@
             pltpu.VMEM((NLB, 2 * LB, 2 * LK), BF16),
         ]
         + [pltpu.VMEM((256, 2 * (hi - lo)), BF16) for lo, hi in RIGHT_SPANS]
-        + [pltpu.SemaphoreType.DMA, pltpu.SMEM((PB * HALO * 2 + 1,), jnp.int32), pltpu.SemaphoreType.DMA((6,)), pltpu.SemaphoreType.DMA((PB,))],
+        + [pltpu.SemaphoreType.DMA, pltpu.SMEM((PB * HALO * 2 + 1,), jnp.int32), pltpu.SemaphoreType.DMA((6,)), pltpu.SemaphoreType.DMA((PB, 4))],
         compiler_params=pltpu.CompilerParams(vmem_limit_bytes=60 * 1024 * 1024),
         name="windows_and_slices",
     )(corners, amp, width, lists, modes, fresnel)

time: 54.4 us -> 54.5 us (level)
  no operation moved by 1% of the time
where the time goes in v5:
time: 54.5 us; the launch traced here: 53.9 us
  Pallas kernels  53.9 us (99%)
    pallas_call x1, Pallas kernels, compute(): pl.pallas_call(compute_kernel, out_shape=jax.ShapeDtypeStruct((PB, 2, W,...  35.5 us
    pallas_call x1, Pallas kernels, gather_lists(): pl.pallas_call(lists_kernel, out_shape=jax.ShapeDtypeStruct((LISTS, PACK,...  18.4 us

profile of v5, /device:TPU:1, one launch (start us, length us, event | category | flops | bytes accessed | tf_op | source)
XLA Modules:
  0.0 53.9 jit_solution(16566704836781322430)
XLA Ops:
  0.0 18.4 %sort_and_gather.1.lists_hbm = s16[36,64,128]{2,1,0:T(8,128)(2,1)} custom-call(s32[2,2048]{1,0:T(2,128)} %bitcast.3, s32[1,2048]{1,0:T(1,128)} %bitcast.4, s32[1,2048]{1,0:T(1,128)} %bitcast.5), custom_call_target="tpu_custom_call" | custom-call | tf_op jit(solution)/shard_map/sort_and_gather/pallas_call | solution.py:539
  18.4 35.5 %windows_and_slices.1 = f32[2,2,512,512]{3,2,1,0:T(8,128)} custom-call(s32[2,2]{1,0:T(2,128)} %corners_hbm.1, f32[4]{0:T(128)} %amp_hbm.1, f32[4]{0:T(128)} %width_hbm.1, s16[36,64,128]{2,1,0:T(8,128)(2,1)} %sort_and_gather.1.lists_hbm, bf16[2,2,512,512]{3,2,1,0:T(8,128)(2,1)} %modes_hbm.1, bf16[2,512,512]{2,1,0:T(8,128)(2,1)} %fresnel_hbm.1), custom_call_target="tpu_custom_call" | custom-call | tf_op jit(solution)/shard_map/windows_and_slices/pallas_call | solution.py:497

commit v6 on v5

--- a/solution.py
+++ b/solution.py
@@ -152,7 +152,7 @@
     local.wait()
 
 
-GR = 32
+GR = 16
 LB = 96
 LK = 128
 NLB = -(-W // LB)
@@ -297,8 +297,9 @@
         rws[b][0:128, k : 2 * k] = -imag
         rws[b][128:256, 0:k] = imag
         rws[b][128:256, k : 2 * k] = real
-    trans0[...] = jnp.zeros_like(trans0)
-    trans1[...] = jnp.zeros_like(trans1)
+    for trans in (trans0, trans1):
+        trans[:, 0:TPAD, :] = jnp.zeros((2, TPAD, W), BF16)
+        trans[:, TPAD + W : TPAD + W + 80, :] = jnp.zeros((2, 80, W), BF16)
 
     out_ref[1] = modes_ref[1].astype(F32)
     copy.wait()

time: 54.5 us -> 55.3 us (1.015)
  the two profiles are of different devices: /device:TPU:1 before, /device:TPU:103 now
where the time goes in v6:
time: 55.3 us; the launch traced here: 55.1 us
  Pallas kernels  55.1 us (100%)
    pallas_call x1, Pallas kernels, compute(): pl.pallas_call(compute_kernel, out_shape=jax.ShapeDtypeStruct((PB, 2, W,...  38.7 us
    pallas_call x1, Pallas kernels, gather_lists(): pl.pallas_call(lists_kernel, out_shape=jax.ShapeDtypeStruct((LISTS, PACK,...  16.5 us

profile of v6, /device:TPU:103, one launch (start us, length us, event | category | flops | bytes accessed | tf_op | source)
XLA Modules:
  0.0 55.1 jit_solution(9890266688715224991)
XLA Ops:
  0.0 16.5 %sort_and_gather.1.lists_hbm = s16[36,64,128]{2,1,0:T(8,128)(2,1)} custom-call(s32[2,2048]{1,0:T(2,128)} %bitcast.3, s32[1,2048]{1,0:T(1,128)} %bitcast.4, s32[1,2048]{1,0:T(1,128)} %bitcast.5), custom_call_target="tpu_custom_call" | custom-call | tf_op jit(solution)/shard_map/sort_and_gather/pallas_call | solution.py:540
  16.5 38.7 %windows_and_slices.1 = f32[2,2,512,512]{3,2,1,0:T(8,128)} custom-call(s32[2,2]{1,0:T(2,128)} %corners_hbm.1, f32[4]{0:T(128)} %amp_hbm.1, f32[4]{0:T(128)} %width_hbm.1, s16[36,64,128]{2,1,0:T(8,128)(2,1)} %sort_and_gather.1.lists_hbm, bf16[2,2,512,512]{3,2,1,0:T(8,128)(2,1)} %modes_hbm.1, bf16[2,512,512]{2,1,0:T(8,128)(2,1)} %fresnel_hbm.1), custom_call_target="tpu_custom_call" | custom-call | tf_op jit(solution)/shard_map/windows_and_slices/pallas_call | solution.py:498
